TPU v7x, 128 devices: a whole 4x4x4 slice. The times are simulated.
128 devices in a mesh: dp: 8 (over x, core), mp: 16 (over z, y).
Axes of the slice: x: 4, y: 4, z: 4, core: 2. Of those that a mesh axis runs over, the one named last changes fastest.
Arguments:
- sensitivity: bfloat16 [8192, 32, 1024], P('dp', 'mp'), may hold values from -0.03125 to 0.03125
- observed: float32 [8192], P('dp'), may hold values from -6 to 6
- row_weight: float32 [8192], P('dp'), may hold values from 1 to 8
- model: float32 [2, 32, 1024], P(None, 'mp'), may hold values from -3 to 3
- smooth_weight: float32 [32, 1024], P('mp'), may hold values from 0.5 to 2
- active: int32 [2, 32, 1024], P(None, 'mp'), may hold values 0 or 1
Outputs:
- update: float32 [2, 32, 1024], P(None, 'mp')
- cg_residual: float32 [2, 32, 1024], P(None, 'mp')
All inputs are finite; a program needn't handle non-finite values. No bound on the sum of `active` on one device may be relied on, other than what follows from the above.
Results may differ from a plain program's by a relative error of at most 0.018.
Values sent between devices are 32-bit elements; how exact they have to be, the bound alone decides.
A program may use at most 64 MiB of HBM per device.

v0:
```python
import jax
import jax.numpy as jnp
from jax import lax
from jax.sharding import PartitionSpec as P

GZ = 16
ITERS = 4


SMOOTHING = 0.25
COUPLING = 0.5


def with_halo(cells, sides, width):
    for axis, dim in sides:
        count = lax.axis_size(axis)
        ends = count - 1
        head = lax.slice_in_dim(cells, 0, width, axis=dim)
        tail = lax.slice_in_dim(cells, cells.shape[dim] - width, cells.shape[dim], axis=dim)
        cells = jnp.concatenate(
            [
                lax.ppermute(tail, axis, [(i, (i + 1) % count) for i in range(ends)]),
                cells,
                lax.ppermute(head, axis, [((i + 1) % count, i) for i in range(ends)]),
            ],
            axis=dim,
        )
    return cells


def from_everyone(x, axis):
    count = lax.axis_size(axis)
    return lax.all_to_all(jnp.broadcast_to(x[None], (count, *x.shape)), axis, 0, 0, tiled=True)


def taken_together(x, axis):
    everything = from_everyone(x, axis)
    return jnp.sum(everything, axis=0)


def inner_sum(field, column_len):
    width = field.shape[-1]
    position = jnp.arange(width) % column_len
    blank_one = jnp.zeros_like(field[..., :1])
    blank_col = jnp.zeros_like(field[..., :column_len])
    later = jnp.where(
        position != column_len - 1, jnp.concatenate([field[..., 1:], blank_one], -1), 0.0
    )
    earlier = jnp.where(position != 0, jnp.concatenate([blank_one, field[..., :-1]], -1), 0.0)
    ahead = jnp.concatenate([field[..., column_len:], blank_col], -1)
    behind = jnp.concatenate([blank_col, field[..., :-column_len]], -1)
    return later + earlier + ahead + behind


def operate(field, smooth_weight):
    padded = with_halo(field, (("mp", 1),), 1)
    beside = padded[:, 2:] + padded[:, :-2] + inner_sum(field, GZ)
    return (
        smooth_weight * field
        + SMOOTHING * (6.0 * field - beside)
        + COUPLING * (field - field[::-1])
    )


def squares(residual):
    return taken_together(jnp.sum(residual * residual), "mp")


def local(sensitivity, observed, row_weight, model, smooth_weight, active):
    rows = sensitivity.shape[0]
    matrix = sensitivity.reshape(rows, -1)
    gravity_rows = lax.axis_index("dp") < lax.axis_size("dp") * 3 // 4
    free_mask = (1.0 - active.astype(jnp.float32)).reshape(2, -1)
    cell_shape = model.shape

    def forward(field):
        flattened = field.reshape(2, -1)
        chosen = jnp.where(gravity_rows, flattened[0], flattened[1]).astype(jnp.bfloat16)
        partial_rows = jnp.dot(matrix, chosen, preferred_element_type=jnp.float32)
        return taken_together(partial_rows, "mp")

    def adjoint(values, regular):
        scaled = (row_weight * values).astype(jnp.bfloat16)
        columns = jnp.dot(scaled, matrix, preferred_element_type=jnp.float32)
        contrib = jnp.stack(
            [jnp.where(gravity_rows, columns, 0.0), jnp.where(gravity_rows, 0.0, columns)]
        )
        regular_flat = regular.reshape(2, -1)
        summed = taken_together(contrib, "dp")
        image = free_mask * (summed + regular_flat)
        return image.reshape(cell_shape)

    predicted = forward(model)
    gradient = adjoint(predicted - observed, operate(model, smooth_weight))
    residual = -gradient
    direction = residual
    solution = jnp.zeros_like(model)
    norm_now = squares(residual)
    for step in range(ITERS):
        image = adjoint(forward(direction), operate(direction, smooth_weight))
        curvature = taken_together(jnp.sum(direction * image), "mp")
        step_len = norm_now / curvature
        solution = solution + step_len * direction
        residual = residual - step_len * image
        norm_next = squares(residual)
        direction = residual + norm_next / norm_now * direction
        norm_now = norm_next
    return (solution, residual)


def solution(mesh):
    return jax.shard_map(
        local,
        mesh=mesh,
        in_specs=(
            P("dp", "mp", None),
            P("dp"),
            P("dp"),
            P(None, "mp", None),
            P("mp", None),
            P(None, "mp", None),
        ),
        out_specs=(P(None, "mp", None), P(None, "mp", None)),
        check_vma=False,
    )
```

profile of v0, /device:TPU:1, one launch (start us, length us, event | category | flops | bytes accessed | tf_op | source)
XLA Modules:
  0.0 284.1 jit_solution(10969849105752143176)
XLA Ops:
  0.6 5.5 %copy.45 = bf16[128,8,2,1024]{3,1,2,0:T(8,128)(2,1)} copy(bf16[128,8,2,1024]{3,2,1,0:T(2,128)(2,1)} %bitcast.72) | data formatting | bytes 8388608
  6.3 3.4 %fusion.70 = f32[1,1024]{1,0:T(1,128)S(1)} fusion(bf16[2048,1]{0,1:T(2,128)(2,1)S(1)} %bitcast.78, bf16[1024,2048]{1,0:T(8,128)(2,1)} %bitcast.62), kind=kOutput, calls=%fused_computation.124 | convolution fusion | flops 4194304 | bytes 4202496 | tf_op jit(solution)/shard_map/dot_general | solution.py:79
  10.3 8.6 %all-to-all-start = ((f32[16,1,1024]{2,1,0:T(1,128)}), f32[16,1,1024]{2,1,0:T(1,128)S(1)}, u32[]{:S(2)}, u32[]{:S(2)}) async-start(f32[16,1,1024]{2,1,0:T(1,128)} %broadcast_in_dim.171), calls=%async_computation | async-start | bytes 131072 | tf_op jit(solution)/shard_map/all_to_all | solution.py:33
  20.2 4.0 %collective-permute-start.1 = (f32[2,1,1024]{2,1,0:T(1,128)S(1)}, f32[2,1,1024]{2,1,0:T(1,128)S(1)}, u32[]{:S(2)}, u32[]{:S(2)}) collective-permute-start(f32[2,1,1024]{2,1,0:T(1,128)S(1)} %get-tuple-element.42), channel_id=1, source_target_pairs={{0,1},{1,2},{2,3},{3,4},{4,5},{5,6},{6,7},{7,8},{8,9},{9,10},{10,1... | collective-permute-start | bytes 24584 | tf_op jit(solution)/shard_map/ppermute | solution.py:22
  29.1 6.4 %all-to-all-start.1 = ((f32[8,2,2048]{2,1,0:T(2,128)}), f32[8,2,2048]{2,1,0:T(2,128)S(1)}, u32[]{:S(2)}, u32[]{:S(2)}) async-start(f32[8,2,2048]{2,1,0:T(2,128)} %broadcast_in_dim.173), calls=%async_computation.1 | async-start | bytes 262144 | tf_op jit(solution)/shard_map/all_to_all | solution.py:33
  35.6 5.2 %all-to-all-done.1 = f32[8,2,2048]{2,1,0:T(2,128)S(1)} async-done(((f32[8,2,2048]{2,1,0:T(2,128)}), f32[8,2,2048]{2,1,0:T(2,128)S(1)}, u32[]{:S(2)}, u32[]{:S(2)}) %all-to-all-start.1) | async-done | bytes 131104 | tf_op jit(solution)/shard_map/all_to_all | solution.py:33
  41.1 3.4 %fusion.72 = f32[1,1024]{1,0:T(1,128)S(1)} fusion(bf16[2048,1]{0,1:T(2,128)(2,1)S(1)} %bitcast.79, bf16[1024,2048]{1,0:T(8,128)(2,1)} %bitcast.64), kind=kOutput, calls=%fused_computation.126 | convolution fusion | flops 4194304 | bytes 4202496 | tf_op jit(solution)/shard_map/dot_general | solution.py:79
  45.2 7.1 %all-to-all-start.3 = ((f32[16,1,1024]{2,1,0:T(1,128)}), f32[16,1,1024]{2,1,0:T(1,128)S(1)}, u32[]{:S(2)}, u32[]{:S(2)}) async-start(f32[16,1,1024]{2,1,0:T(1,128)} %broadcast_in_dim.178), calls=%async_computation.3 | async-start | bytes 131072 | tf_op jit(solution)/shard_map/all_to_all | solution.py:33
  53.6 4.0 %collective-permute-start.3 = (f32[2,1,1024]{2,1,0:T(1,128)S(1)}, f32[2,1,1024]{2,1,0:T(1,128)S(1)}, u32[]{:S(2)}, u32[]{:S(2)}) collective-permute-start(f32[2,1,1024]{2,1,0:T(1,128)S(1)} %get-tuple-element.36), channel_id=1, source_target_pairs={{0,1},{1,2},{2,3},{3,4},{4,5},{5,6},{6,7},{7,8},{8,9},{9,10},{10,1... | collective-permute-start | bytes 24584 | tf_op jit(solution)/shard_map/ppermute | solution.py:22
  62.4 5.6 %all-to-all-start.4 = ((f32[8,2,2048]{2,1,0:T(2,128)}), f32[8,2,2048]{2,1,0:T(2,128)S(1)}, u32[]{:S(2)}, u32[]{:S(2)}) async-start(f32[8,2,2048]{2,1,0:T(2,128)} %broadcast_in_dim.179), calls=%async_computation.4 | async-start | bytes 262144 | tf_op jit(solution)/shard_map/all_to_all | solution.py:33
  68.0 5.2 %all-to-all-done.4 = f32[8,2,2048]{2,1,0:T(2,128)S(1)} async-done(((f32[8,2,2048]{2,1,0:T(2,128)}), f32[8,2,2048]{2,1,0:T(2,128)S(1)}, u32[]{:S(2)}, u32[]{:S(2)}) %all-to-all-start.4) | async-done | bytes 131104 | tf_op jit(solution)/shard_map/all_to_all | solution.py:33
  74.7 13.2 %all_to_all.103 = f32[16,1,1]{2,1,0:T(1,128)S(1)} all-to-all(f32[16,1,1]{2,1,0:T(1,128)S(1)} %broadcast_in_dim.177), channel_id=1, replica_groups=mesh['dp'=8,'mp'=16] {'mp'}, dimensions={0} | all-to-all | bytes 128 | tf_op jit(solution)/shard_map/all_to_all | solution.py:33
  89.2 3.5 %all-to-all-start.5 = ((f32[16,1,1]{2,1,0:T(1,128)}), f32[16,1,1]{2,1,0:T(1,128)S(1)}, u32[]{:S(2)}, u32[]{:S(2)}) async-start(f32[16,1,1]{2,1,0:T(1,128)} %broadcast_in_dim.180), calls=%async_computation.5 | async-start | bytes 16384 | tf_op jit(solution)/shard_map/all_to_all | solution.py:33
  93.3 5.6 %all-to-all-done.5 = f32[16,1,1]{2,1,0:T(1,128)S(1)} async-done(((f32[16,1,1]{2,1,0:T(1,128)}), f32[16,1,1]{2,1,0:T(1,128)S(1)}, u32[]{:S(2)}, u32[]{:S(2)}) %all-to-all-start.5) | async-done | bytes 96 | tf_op jit(solution)/shard_map/all_to_all | solution.py:33
  102.2 9.1 %all_to_all.104 = f32[16,1,1]{2,1,0:T(1,128)S(1)} all-to-all(f32[16,1,1]{2,1,0:T(1,128)S(1)} %broadcast_in_dim.181), channel_id=1, replica_groups=mesh['dp'=8,'mp'=16] {'mp'}, dimensions={0} | all-to-all | bytes 128 | tf_op jit(solution)/shard_map/all_to_all | solution.py:33
  117.5 3.5 %all-to-all-start.7 = ((f32[16,1,1024]{2,1,0:T(1,128)}), f32[16,1,1024]{2,1,0:T(1,128)S(1)}, u32[]{:S(2)}, u32[]{:S(2)}) async-start(f32[16,1,1024]{2,1,0:T(1,128)} %broadcast_in_dim.182), calls=%async_computation.7 | async-start | bytes 131072 | tf_op jit(solution)/shard_map/all_to_all | solution.py:33
  122.3 4.0 %collective-permute-start.5 = (f32[2,1,1024]{2,1,0:T(1,128)S(1)}, f32[2,1,1024]{2,1,0:T(1,128)S(1)}, u32[]{:S(2)}, u32[]{:S(2)}) collective-permute-start(f32[2,1,1024]{2,1,0:T(1,128)S(1)} %get-tuple-element.30), channel_id=1, source_target_pairs={{0,1},{1,2},{2,3},{3,4},{4,5},{5,6},{6,7},{7,8},{8,9},{9,10},{10,1... | collective-permute-start | bytes 24584 | tf_op jit(solution)/shard_map/ppermute | solution.py:22
  131.1 9.3 %all-to-all-start.8 = ((f32[8,2,2048]{2,1,0:T(2,128)}), f32[8,2,2048]{2,1,0:T(2,128)S(1)}, u32[]{:S(2)}, u32[]{:S(2)}) async-start(f32[8,2,2048]{2,1,0:T(2,128)} %broadcast_in_dim.183), calls=%async_computation.8 | async-start | bytes 262144 | tf_op jit(solution)/shard_map/all_to_all | solution.py:33
  140.4 5.2 %all-to-all-done.8 = f32[8,2,2048]{2,1,0:T(2,128)S(1)} async-done(((f32[8,2,2048]{2,1,0:T(2,128)}), f32[8,2,2048]{2,1,0:T(2,128)S(1)}, u32[]{:S(2)}, u32[]{:S(2)}) %all-to-all-start.8) | async-done | bytes 131104 | tf_op jit(solution)/shard_map/all_to_all | solution.py:33
  147.1 13.2 %all_to_all.105 = f32[16,1,1]{2,1,0:T(1,128)S(1)} all-to-all(f32[16,1,1]{2,1,0:T(1,128)S(1)} %broadcast_in_dim.184), channel_id=1, replica_groups=mesh['dp'=8,'mp'=16] {'mp'}, dimensions={0} | all-to-all | bytes 128 | tf_op jit(solution)/shard_map/all_to_all | solution.py:33
  163.5 9.1 %all_to_all.106 = f32[16,1,1]{2,1,0:T(1,128)S(1)} all-to-all(f32[16,1,1]{2,1,0:T(1,128)S(1)} %broadcast_in_dim.185), channel_id=1, replica_groups=mesh['dp'=8,'mp'=16] {'mp'}, dimensions={0} | all-to-all | bytes 128 | tf_op jit(solution)/shard_map/all_to_all | solution.py:33
  178.8 3.5 %all-to-all-start.11 = ((f32[16,1,1024]{2,1,0:T(1,128)}), f32[16,1,1024]{2,1,0:T(1,128)S(1)}, u32[]{:S(2)}, u32[]{:S(2)}) async-start(f32[16,1,1024]{2,1,0:T(1,128)} %broadcast_in_dim.186), calls=%async_computation.11 | async-start | bytes 131072 | tf_op jit(solution)/shard_map/all_to_all | solution.py:33
  183.6 4.2 %collective-permute-start.7 = (f32[2,1,1024]{2,1,0:T(1,128)S(1)}, f32[2,1,1024]{2,1,0:T(1,128)S(1)}, u32[]{:S(2)}, u32[]{:S(2)}) collective-permute-start(f32[2,1,1024]{2,1,0:T(1,128)S(1)} %get-tuple-element.24), channel_id=1, source_target_pairs={{0,1},{1,2},{2,3},{3,4},{4,5},{5,6},{6,7},{7,8},{8,9},{9,10},{10,1... | collective-permute-start | bytes 24584 | tf_op jit(solution)/shard_map/ppermute | solution.py:22
  192.4 8.1 %all-to-all-start.12 = ((f32[8,2,2048]{2,1,0:T(2,128)}), f32[8,2,2048]{2,1,0:T(2,128)S(1)}, u32[]{:S(2)}, u32[]{:S(2)}) async-start(f32[8,2,2048]{2,1,0:T(2,128)} %broadcast_in_dim.187), calls=%async_computation.12 | async-start | bytes 262144 | tf_op jit(solution)/shard_map/all_to_all | solution.py:33
  200.6 5.2 %all-to-all-done.12 = f32[8,2,2048]{2,1,0:T(2,128)S(1)} async-done(((f32[8,2,2048]{2,1,0:T(2,128)}), f32[8,2,2048]{2,1,0:T(2,128)S(1)}, u32[]{:S(2)}, u32[]{:S(2)}) %all-to-all-start.12) | async-done | bytes 131104 | tf_op jit(solution)/shard_map/all_to_all | solution.py:33
  207.3 13.4 %all_to_all.107 = f32[16,1,1]{2,1,0:T(1,128)S(1)} all-to-all(f32[16,1,1]{2,1,0:T(1,128)S(1)} %broadcast_in_dim.188), channel_id=1, replica_groups=mesh['dp'=8,'mp'=16] {'mp'}, dimensions={0} | all-to-all | bytes 128 | tf_op jit(solution)/shard_map/all_to_all | solution.py:33
  223.9 9.1 %all_to_all.108 = f32[16,1,1]{2,1,0:T(1,128)S(1)} all-to-all(f32[16,1,1]{2,1,0:T(1,128)S(1)} %broadcast_in_dim.189), channel_id=1, replica_groups=mesh['dp'=8,'mp'=16] {'mp'}, dimensions={0} | all-to-all | bytes 128 | tf_op jit(solution)/shard_map/all_to_all | solution.py:33
  239.2 3.5 %all-to-all-start.15 = ((f32[16,1,1024]{2,1,0:T(1,128)}), f32[16,1,1024]{2,1,0:T(1,128)S(1)}, u32[]{:S(2)}, u32[]{:S(2)}) async-start(f32[16,1,1024]{2,1,0:T(1,128)} %broadcast_in_dim.190), calls=%async_computation.15 | async-start | bytes 131072 | tf_op jit(solution)/shard_map/all_to_all | solution.py:33
  244.0 4.0 %collective-permute-start.9 = (f32[2,1,1024]{2,1,0:T(1,128)S(1)}, f32[2,1,1024]{2,1,0:T(1,128)S(1)}, u32[]{:S(2)}, u32[]{:S(2)}) collective-permute-start(f32[2,1,1024]{2,1,0:T(1,128)S(1)} %get-tuple-element.18), channel_id=1, source_target_pairs={{0,1},{1,2},{2,3},{3,4},{4,5},{5,6},{6,7},{7,8},{8,9},{9,10},{10,1... | collective-permute-start | bytes 24584 | tf_op jit(solution)/shard_map/ppermute | solution.py:22
  252.8 8.1 %all-to-all-start.16 = ((f32[8,2,2048]{2,1,0:T(2,128)}), f32[8,2,2048]{2,1,0:T(2,128)S(1)}, u32[]{:S(2)}, u32[]{:S(2)}) async-start(f32[8,2,2048]{2,1,0:T(2,128)} %broadcast_in_dim.191), calls=%async_computation.16 | async-start | bytes 262144 | tf_op jit(solution)/shard_map/all_to_all | solution.py:33
  261.0 5.2 %all-to-all-done.16 = f32[8,2,2048]{2,1,0:T(2,128)S(1)} async-done(((f32[8,2,2048]{2,1,0:T(2,128)}), f32[8,2,2048]{2,1,0:T(2,128)S(1)}, u32[]{:S(2)}, u32[]{:S(2)}) %all-to-all-start.16) | async-done | bytes 131104 | tf_op jit(solution)/shard_map/all_to_all | solution.py:33
  267.7 13.2 %all_to_all.109 = f32[16,1,1]{2,1,0:T(1,128)S(1)} all-to-all(f32[16,1,1]{2,1,0:T(1,128)S(1)} %broadcast_in_dim.192), channel_id=1, replica_groups=mesh['dp'=8,'mp'=16] {'mp'}, dimensions={0} | all-to-all | bytes 128 | tf_op jit(solution)/shard_map/all_to_all | solution.py:33
  (138 shorter events, 61.9 us)
Async XLA Ops:
  0.6 5.6 %copy-start = (f32[2,2,1024]{2,1,0:T(2,128)S(1)}, f32[2,2,1024]{2,1,0:T(2,128)}, u32[]{:S(2)}) copy-start(f32[2,2,1024]{2,1,0:T(2,128)} %param.9) | copy-start | bytes 49156
  6.2 19.3 %copy-start.3 = (f32[1024]{0:T(1024)S(1)}, f32[1024]{0:T(1024)}, u32[]{:S(2)}) copy-start(f32[1024]{0:T(1024)} %param.8) | copy-start | bytes 12292
  6.2 19.3 %copy-start.4 = (f32[1024]{0:T(1024)S(1)}, f32[1024]{0:T(1024)}, u32[]{:S(2)}) copy-start(f32[1024]{0:T(1024)} %param.7) | copy-start | bytes 12292
  6.2 34.6 %copy-start.1 = (s32[2,2,1024]{2,1,0:T(2,128)S(1)}, s32[2,2,1024]{2,1,0:T(2,128)}, u32[]{:S(2)}) copy-start(s32[2,2,1024]{2,1,0:T(2,128)} %param.11) | copy-start | bytes 49156
  6.2 34.6 %copy-start.2 = (f32[2,1024]{1,0:T(2,128)S(1)}, f32[2,1024]{1,0:T(2,128)}, u32[]{:S(2)}) copy-start(f32[2,1024]{1,0:T(2,128)} %param.10) | copy-start | bytes 24580
  10.3 15.1 %all-to-all-start = ((f32[16,1,1024]{2,1,0:T(1,128)}), f32[16,1,1024]{2,1,0:T(1,128)S(1)}, u32[]{:S(2)}, u32[]{:S(2)}) async-start(f32[16,1,1024]{2,1,0:T(1,128)} %broadcast_in_dim.171), calls=%async_computation | async-start | bytes 131072 | tf_op jit(solution)/shard_map/all_to_all | solution.py:33
  18.9 21.9 %collective-permute-start = (f32[2,1,1024]{2,1,0:T(1,128)S(1)}, f32[2,1,1024]{2,1,0:T(1,128)S(1)}, u32[]{:S(2)}, u32[]{:S(2)}) collective-permute-start(f32[2,1,1024]{2,1,0:T(1,128)S(1)} %get-tuple-element.41), channel_id=1, source_target_pairs={{1,0},{2,1},{3,2},{4,3},{5,4},{6,5},{7,6},{8,7},{9,8},{10,9},{11,1... | collective-permute-start | bytes 24584 | tf_op jit(solution)/shard_map/ppermute | solution.py:24
  20.2 20.6 %collective-permute-start.1 = (f32[2,1,1024]{2,1,0:T(1,128)S(1)}, f32[2,1,1024]{2,1,0:T(1,128)S(1)}, u32[]{:S(2)}, u32[]{:S(2)}) collective-permute-start(f32[2,1,1024]{2,1,0:T(1,128)S(1)} %get-tuple-element.42), channel_id=1, source_target_pairs={{0,1},{1,2},{2,3},{3,4},{4,5},{5,6},{6,7},{7,8},{8,9},{9,10},{10,1... | collective-permute-start | bytes 24584 | tf_op jit(solution)/shard_map/ppermute | solution.py:22
  29.1 11.7 %all-to-all-start.1 = ((f32[8,2,2048]{2,1,0:T(2,128)}), f32[8,2,2048]{2,1,0:T(2,128)S(1)}, u32[]{:S(2)}, u32[]{:S(2)}) async-start(f32[8,2,2048]{2,1,0:T(2,128)} %broadcast_in_dim.173), calls=%async_computation.1 | async-start | bytes 262144 | tf_op jit(solution)/shard_map/all_to_all | solution.py:33
  45.2 13.6 %all-to-all-start.3 = ((f32[16,1,1024]{2,1,0:T(1,128)}), f32[16,1,1024]{2,1,0:T(1,128)S(1)}, u32[]{:S(2)}, u32[]{:S(2)}) async-start(f32[16,1,1024]{2,1,0:T(1,128)} %broadcast_in_dim.178), calls=%async_computation.3 | async-start | bytes 131072 | tf_op jit(solution)/shard_map/all_to_all | solution.py:33
  52.3 21.1 %collective-permute-start.2 = (f32[2,1,1024]{2,1,0:T(1,128)S(1)}, f32[2,1,1024]{2,1,0:T(1,128)S(1)}, u32[]{:S(2)}, u32[]{:S(2)}) collective-permute-start(f32[2,1,1024]{2,1,0:T(1,128)S(1)} %get-tuple-element.35), channel_id=1, source_target_pairs={{1,0},{2,1},{3,2},{4,3},{5,4},{6,5},{7,6},{8,7},{9,8},{10,9},{11,1... | collective-permute-start | bytes 24584 | tf_op jit(solution)/shard_map/ppermute | solution.py:24
  53.6 19.8 %collective-permute-start.3 = (f32[2,1,1024]{2,1,0:T(1,128)S(1)}, f32[2,1,1024]{2,1,0:T(1,128)S(1)}, u32[]{:S(2)}, u32[]{:S(2)}) collective-permute-start(f32[2,1,1024]{2,1,0:T(1,128)S(1)} %get-tuple-element.36), channel_id=1, source_target_pairs={{0,1},{1,2},{2,3},{3,4},{4,5},{5,6},{6,7},{7,8},{8,9},{9,10},{10,1... | collective-permute-start | bytes 24584 | tf_op jit(solution)/shard_map/ppermute | solution.py:22
  62.4 10.9 %all-to-all-start.4 = ((f32[8,2,2048]{2,1,0:T(2,128)}), f32[8,2,2048]{2,1,0:T(2,128)S(1)}, u32[]{:S(2)}, u32[]{:S(2)}) async-start(f32[8,2,2048]{2,1,0:T(2,128)} %broadcast_in_dim.179), calls=%async_computation.4 | async-start | bytes 262144 | tf_op jit(solution)/shard_map/all_to_all | solution.py:33
  89.2 9.7 %all-to-all-start.5 = ((f32[16,1,1]{2,1,0:T(1,128)}), f32[16,1,1]{2,1,0:T(1,128)S(1)}, u32[]{:S(2)}, u32[]{:S(2)}) async-start(f32[16,1,1]{2,1,0:T(1,128)} %broadcast_in_dim.180), calls=%async_computation.5 | async-start | bytes 16384 | tf_op jit(solution)/shard_map/all_to_all | solution.py:33
  117.5 10.0 %all-to-all-start.7 = ((f32[16,1,1024]{2,1,0:T(1,128)}), f32[16,1,1024]{2,1,0:T(1,128)S(1)}, u32[]{:S(2)}, u32[]{:S(2)}) async-start(f32[16,1,1024]{2,1,0:T(1,128)} %broadcast_in_dim.182), calls=%async_computation.7 | async-start | bytes 131072 | tf_op jit(solution)/shard_map/all_to_all | solution.py:33
  121.0 24.7 %collective-permute-start.4 = (f32[2,1,1024]{2,1,0:T(1,128)S(1)}, f32[2,1,1024]{2,1,0:T(1,128)S(1)}, u32[]{:S(2)}, u32[]{:S(2)}) collective-permute-start(f32[2,1,1024]{2,1,0:T(1,128)S(1)} %get-tuple-element.29), channel_id=1, source_target_pairs={{1,0},{2,1},{3,2},{4,3},{5,4},{6,5},{7,6},{8,7},{9,8},{10,9},{11,1... | collective-permute-start | bytes 24584 | tf_op jit(solution)/shard_map/ppermute | solution.py:24
  122.3 23.4 %collective-permute-start.5 = (f32[2,1,1024]{2,1,0:T(1,128)S(1)}, f32[2,1,1024]{2,1,0:T(1,128)S(1)}, u32[]{:S(2)}, u32[]{:S(2)}) collective-permute-start(f32[2,1,1024]{2,1,0:T(1,128)S(1)} %get-tuple-element.30), channel_id=1, source_target_pairs={{0,1},{1,2},{2,3},{3,4},{4,5},{5,6},{6,7},{7,8},{8,9},{9,10},{10,1... | collective-permute-start | bytes 24584 | tf_op jit(solution)/shard_map/ppermute | solution.py:22
  131.1 14.6 %all-to-all-start.8 = ((f32[8,2,2048]{2,1,0:T(2,128)}), f32[8,2,2048]{2,1,0:T(2,128)S(1)}, u32[]{:S(2)}, u32[]{:S(2)}) async-start(f32[8,2,2048]{2,1,0:T(2,128)} %broadcast_in_dim.183), calls=%async_computation.8 | async-start | bytes 262144 | tf_op jit(solution)/shard_map/all_to_all | solution.py:33
  178.8 10.0 %all-to-all-start.11 = ((f32[16,1,1024]{2,1,0:T(1,128)}), f32[16,1,1024]{2,1,0:T(1,128)S(1)}, u32[]{:S(2)}, u32[]{:S(2)}) async-start(f32[16,1,1024]{2,1,0:T(1,128)} %broadcast_in_dim.186), calls=%async_computation.11 | async-start | bytes 131072 | tf_op jit(solution)/shard_map/all_to_all | solution.py:33
  182.3 23.6 %collective-permute-start.6 = (f32[2,1,1024]{2,1,0:T(1,128)S(1)}, f32[2,1,1024]{2,1,0:T(1,128)S(1)}, u32[]{:S(2)}, u32[]{:S(2)}) collective-permute-start(f32[2,1,1024]{2,1,0:T(1,128)S(1)} %get-tuple-element.23), channel_id=1, source_target_pairs={{1,0},{2,1},{3,2},{4,3},{5,4},{6,5},{7,6},{8,7},{9,8},{10,9},{11,1... | collective-permute-start | bytes 24584 | tf_op jit(solution)/shard_map/ppermute | solution.py:24
  183.6 22.3 %collective-permute-start.7 = (f32[2,1,1024]{2,1,0:T(1,128)S(1)}, f32[2,1,1024]{2,1,0:T(1,128)S(1)}, u32[]{:S(2)}, u32[]{:S(2)}) collective-permute-start(f32[2,1,1024]{2,1,0:T(1,128)S(1)} %get-tuple-element.24), channel_id=1, source_target_pairs={{0,1},{1,2},{2,3},{3,4},{4,5},{5,6},{6,7},{7,8},{8,9},{9,10},{10,1... | collective-permute-start | bytes 24584 | tf_op jit(solution)/shard_map/ppermute | solution.py:22
  192.4 13.4 %all-to-all-start.12 = ((f32[8,2,2048]{2,1,0:T(2,128)}), f32[8,2,2048]{2,1,0:T(2,128)S(1)}, u32[]{:S(2)}, u32[]{:S(2)}) async-start(f32[8,2,2048]{2,1,0:T(2,128)} %broadcast_in_dim.187), calls=%async_computation.12 | async-start | bytes 262144 | tf_op jit(solution)/shard_map/all_to_all | solution.py:33
  239.2 10.0 %all-to-all-start.15 = ((f32[16,1,1024]{2,1,0:T(1,128)}), f32[16,1,1024]{2,1,0:T(1,128)S(1)}, u32[]{:S(2)}, u32[]{:S(2)}) async-start(f32[16,1,1024]{2,1,0:T(1,128)} %broadcast_in_dim.190), calls=%async_computation.15 | async-start | bytes 131072 | tf_op jit(solution)/shard_map/all_to_all | solution.py:33
  242.7 23.6 %collective-permute-start.8 = (f32[2,1,1024]{2,1,0:T(1,128)S(1)}, f32[2,1,1024]{2,1,0:T(1,128)S(1)}, u32[]{:S(2)}, u32[]{:S(2)}) collective-permute-start(f32[2,1,1024]{2,1,0:T(1,128)S(1)} %get-tuple-element.17), channel_id=1, source_target_pairs={{1,0},{2,1},{3,2},{4,3},{5,4},{6,5},{7,6},{8,7},{9,8},{10,9},{11,1... | collective-permute-start | bytes 24584 | tf_op jit(solution)/shard_map/ppermute | solution.py:24
  244.0 22.3 %collective-permute-start.9 = (f32[2,1,1024]{2,1,0:T(1,128)S(1)}, f32[2,1,1024]{2,1,0:T(1,128)S(1)}, u32[]{:S(2)}, u32[]{:S(2)}) collective-permute-start(f32[2,1,1024]{2,1,0:T(1,128)S(1)} %get-tuple-element.18), channel_id=1, source_target_pairs={{0,1},{1,2},{2,3},{3,4},{4,5},{5,6},{6,7},{7,8},{8,9},{9,10},{10,1... | collective-permute-start | bytes 24584 | tf_op jit(solution)/shard_map/ppermute | solution.py:22
  252.8 13.4 %all-to-all-start.16 = ((f32[8,2,2048]{2,1,0:T(2,128)}), f32[8,2,2048]{2,1,0:T(2,128)S(1)}, u32[]{:S(2)}, u32[]{:S(2)}) async-start(f32[8,2,2048]{2,1,0:T(2,128)} %broadcast_in_dim.191), calls=%async_computation.16 | async-start | bytes 262144 | tf_op jit(solution)/shard_map/all_to_all | solution.py:33
where the time goes:
time: 287 us; the launch traced here: 284 us
  starting transfers between devices  93.7 us (33%)
  blocking collectives  80.3 us (28%)
  waiting for transfers between devices  37.3 us (13%)
  matrix products  31.1 us (11%)
  local copies, waits for them, and re-layouts  19.3 us (7%)
  other arithmetic  11.8 us (4%)
  between operations  10.6 us (4%)
    all_to_all x7, blocking collectives, from_everyone(): lax.all_to_all(jnp.broadcast_to(x[None], (count, *x.shape)), axis, 0, 0,...  80.3 us
    all_to_all x11, starting transfers between devices, from_everyone(): lax.all_to_all(jnp.broadcast_to(x[None], (count, *x.shape)), axis, 0, 0,...  67.2 us
    all_to_all x11, waiting for transfers between devices, from_everyone(): lax.all_to_all(jnp.broadcast_to(x[None], (count, *x.shape)), axis, 0, 0,...  37.2 us
    ppermute x5, starting transfers between devices, with_halo(): lax.ppermute(tail, axis, [(i, (i + 1) % count) for i in range(ends)])  20.1 us
    dot_general x5, matrix products, forward(): partial_rows = jnp.dot(matrix, chosen, preferred_element_type=jnp.float32)  16.8 us
    dot_general x5, matrix products, adjoint(): columns = jnp.dot(scaled, matrix, preferred_element_type=jnp.float32)  14.2 us
    broadcast_in_dim x18, local copies, waits for them, and re-layouts, from_everyone(): jnp.broadcast_to(x[None], (count, *x.shape))  12.6 us
    ppermute x5, starting transfers between devices, with_halo(): lax.ppermute(head, axis, [((i + 1) % count, i) for i in range(ends)])  6.46 us
  transfers between devices with their start and end apart: 21, of which 11 were waited for; matrix products, arithmetic and copies ran while one was open for 7% of the time, Pallas kernels for 0%

commit v1 on v0

v1 whole, which is shorter than its diff:
```python
import functools

import jax
import jax.numpy as jnp
from jax import lax
from jax.experimental import pallas as pl
from jax.experimental.pallas import tpu as pltpu
from jax.sharding import PartitionSpec as P

MESH = pl.DeviceIdType.MESH
F32 = jnp.float32
BF16 = jnp.bfloat16

GZ = 16
STEPS = 5
SMOOTHING = 0.25
COUPLING = 0.5

ROWS = 1024
CELLS = 2048
CHUNK = 128
CHUNKS = ROWS // CHUNK
DP = 8
MP = 16
MROWS = 9


def spread(tiles):
    parts = []
    for tile in tiles:
        high = tile.astype(BF16).astype(F32)
        low = tile - high
        for c in range(8):
            both = jnp.concatenate(
                [
                    jnp.broadcast_to(high[c : c + 1], (8, 128)),
                    jnp.broadcast_to(low[c : c + 1], (8, 128)),
                ],
                axis=0,
            )
            parts.append(both.astype(BF16))
    return jnp.concatenate(parts, axis=1)


def gathered(product, first):
    total = product[:8] + product[8:]
    sub = lax.broadcasted_iota(jnp.int32, (8, 128), 0)
    tile = jnp.zeros((8, 128), F32)
    for c in range(8):
        at = (first + c) * 128
        tile = jnp.where(sub == c, total[:, at : at + 128], tile)
    return tile


def regular(u, below, above, weight):
    lane = lax.broadcasted_iota(jnp.int32, (8, 128), 1)
    sub = lax.broadcasted_iota(jnp.int32, (8, 128), 0)
    outs = []
    for layer in range(2):
        for field in range(2):
            v = u[layer * 2 + field]
            beside = u[(1 - layer) * 2 + field] + (below[field] if layer == 0 else above[field])
            beside += jnp.where(lane % GZ != GZ - 1, pltpu.roll(v, 127, 1), 0.0)
            beside += jnp.where(lane % GZ != 0, pltpu.roll(v, 1, 1), 0.0)
            later = pltpu.roll(v, 128 - GZ, 1)
            wrapped = jnp.where(sub < 7, pltpu.roll(later, 7, 0), 0.0)
            beside += jnp.where(lane < 128 - GZ, later, wrapped)
            earlier = pltpu.roll(v, GZ, 1)
            wrapped = jnp.where(sub > 0, pltpu.roll(earlier, 1, 0), 0.0)
            beside += jnp.where(lane >= GZ, earlier, wrapped)
            other = u[layer * 2 + 1 - field]
            outs.append(weight[layer] * v + SMOOTHING * (6.0 * v - beside) + COUPLING * (v - other))
    return jnp.stack(outs)


def lanes_of(cells):
    return jnp.sum(jnp.sum(cells, axis=0), axis=0, keepdims=True)


def two_sums(one, two):
    lane = lax.broadcasted_iota(jnp.int32, (1, 128), 1)
    return jnp.where(lane < 64, one + pltpu.roll(one, 64, 1), two + pltpu.roll(two, 64, 1))


def split_sums(row):
    lane = lax.broadcasted_iota(jnp.int32, (1, 128), 1)
    one = jnp.sum(jnp.where(lane < 64, row, 0.0), axis=1, keepdims=True)
    two = jnp.sum(jnp.where(lane < 64, 0.0, row), axis=1, keepdims=True)
    return one, two


def kernel(
    x_ref, obs_ref, rw_ref, model_ref, smooth_ref, active_ref,
    upd_ref, res_ref,
    raw, wide, md, mt, mbuf, dbuf, ubuf, halo, smbuf, sdbuf,
    free, weight, x_s, r_s, p_s, s_s, z_s, rs_s, rr_s, base, coef, fs_s, fr_s, scal,
    load_sem, m_send, m_recv, d_send, d_recv, h_send, h_recv, s_send, s_recv,
):
    dp = lax.axis_index("dp")
    mp = lax.axis_index("mp")
    gravity = dp < DP * 3 // 4

    loads = [
        pltpu.make_async_copy(
            x_ref.at[pl.ds(k * CHUNK * 16, CHUNK * 16)],
            raw.at[pl.ds(k * CHUNK * 16, CHUNK * 16)],
            load_sem.at[k],
        )
        for k in range(CHUNKS)
    ]
    for load in loads:
        load.start()

    m_peers = [{"dp": dp, "mp": lax.rem(mp + k, MP)} for k in range(1, MP)]
    d_peers = [{"dp": lax.rem(dp + k, DP), "mp": mp} for k in range(1, DP)]
    barrier = pltpu.get_barrier_semaphore()
    for peer in m_peers + d_peers:
        pl.semaphore_signal(barrier, inc=1, device_id=peer, device_id_type=MESH)

    for layer in range(2):
        weight[layer] = smooth_ref[pl.ds(layer, 8, stride=2), :]
        for field in range(2):
            at = pl.ds(field * 16 + layer, 8, stride=2)
            ubuf[0, layer * 2 + field] = model_ref[at, :]
            free[layer * 2 + field] = 1.0 - active_ref[at, :].astype(F32)
    for ref in (x_s, p_s, s_s, z_s, rs_s):
        ref[...] = jnp.zeros_like(ref)
    fs_s[...] = jnp.zeros_like(fs_s)

    def chosen(u):
        return [jnp.where(gravity, u[layer * 2], u[layer * 2 + 1]) for layer in range(2)]

    left = spread(chosen(ubuf[0]))
    for k in range(CHUNKS):
        loads[k].wait()
        wide[...] = raw[pl.ds(k * CHUNK * 16, CHUNK * 16), :].astype(F32)
        for c in range(8):
            for layer in range(2):
                at = (layer * 8 + c) * 128
                part = wide[pl.ds(c * 2 + layer, CHUNK, stride=16), :]
                md[pl.ds(k * CHUNK, CHUNK), at : at + 128] = part.astype(BF16)
        some = lax.dot_general(
            left, md[pl.ds(k * CHUNK, CHUNK), :], (((1,), (1,)), ((), ())), preferred_element_type=F32
        )
        mbuf[0, mp, k : k + 1, :] = some[0:1] + some[8:9]
    mbuf[0, mp, 8:9, :] = jnp.zeros((1, 128), F32)

    pl.semaphore_wait(barrier, MP - 1 + DP - 1)

    def step(k, carry):
        now = lax.rem(k, 2)
        later = 1 - now

        mine = mbuf.at[now, mp, pl.ds(0, MROWS)]
        for peer in m_peers:
            pltpu.make_async_remote_copy(
                src_ref=mine, dst_ref=mine, send_sem=m_send.at[now], recv_sem=m_recv.at[now],
                device_id=peer, device_id_type=MESH,
            ).start()
        halo_copies = []
        for side, (first, peer) in enumerate(
            [(2, {"dp": dp, "mp": lax.rem(mp + 1, MP)}), (0, {"dp": dp, "mp": lax.rem(mp + MP - 1, MP)})]
        ):
            copy = pltpu.make_async_remote_copy(
                src_ref=ubuf.at[now, pl.ds(first, 2)], dst_ref=halo.at[now, side],
                send_sem=h_send.at[side], recv_sem=h_recv.at[now, side],
                device_id=peer, device_id_type=MESH,
            )
            copy.start()
            halo_copies.append(copy)

        @pl.when(k == 0)
        def _():
            row = lax.broadcasted_iota(jnp.int32, (256, 256), 0)
            col = lax.broadcasted_iota(jnp.int32, (256, 256), 1)
            eye = jnp.where(row == col, 1.0, 0.0).astype(BF16)

            def turn(j, carry):
                at = pl.multiple_of(j * 256, 256)
                turned = lax.dot_general(
                    eye, md[:, pl.ds(at, 256)], (((1,), (1,)), ((), ())), preferred_element_type=F32
                )
                mt[pl.ds(at, 256), :] = turned.astype(BF16)
                return carry

            lax.fori_loop(0, CELLS // 256, turn, 0)

        all_m = mbuf.at[now, pl.ds(0, MP - 1), pl.ds(0, MROWS)]
        pltpu.make_async_copy(all_m, all_m, m_recv.at[now]).wait()
        rows = mbuf[now, 0, 0:8]
        sums = mbuf[now, 0, 8:9]
        for j in range(1, MP):
            rows += mbuf[now, j, 0:8]
            sums += mbuf[now, j, 8:9]

        scaled = rw_ref[...] * (rows - jnp.where(k == 0, obs_ref[...], 0.0))
        product = jnp.dot(spread([scaled]), md[...], preferred_element_type=F32)
        dbuf[now, dp, 0:8] = gathered(product, 0)
        dbuf[now, dp, 8:16] = gathered(product, 8)
        mine_d = dbuf.at[now, dp]
        for peer in d_peers:
            pltpu.make_async_remote_copy(
                src_ref=mine_d, dst_ref=mine_d, send_sem=d_send.at[now], recv_sem=d_recv.at[now],
                device_id=peer, device_id_type=MESH,
            ).start()

        for copy in halo_copies:
            copy.wait()
        u = ubuf[now]
        below = jnp.where(mp > 0, halo[now, 0], 0.0)
        above = jnp.where(mp < MP - 1, halo[now, 1], 0.0)
        smooth = regular(u, below, above, weight[...])
        mask = free[...]

        @pl.when(k == 0)
        def _():
            base[...] = -(mask * smooth)
            coef[...] = -mask

        @pl.when(k == 1)
        def _():
            r_s[...] = u
            fr_s[...] = rows
            rr_s[...] = smooth
            base[...] = mask * smooth
            coef[...] = mask

        @pl.when(k >= 2)
        def _():
            gamma, delta = split_sums(sums)
            first = k == 2
            beta = jnp.where(first, 0.0, gamma / jnp.where(first, 1.0, scal[0, 0:1, 0:1]))
            past = beta * gamma / jnp.where(first, 1.0, scal[1, 0:1, 0:1])
            alpha = gamma / (delta - past)
            scal[0] = jnp.broadcast_to(gamma, (8, 128))
            scal[1] = jnp.broadcast_to(alpha, (8, 128))
            r = r_s[...]
            p = r + beta * p_s[...]
            s = u + beta * s_s[...]
            r = r - alpha * s
            p_s[...] = p
            s_s[...] = s
            r_s[...] = r
            x_s[...] = x_s[...] + alpha * p
            fs = rows + beta * fs_s[...]
            fr = fr_s[...] - alpha * fs
            fs_s[...] = fs
            fr_s[...] = fr
            rs = smooth + beta * rs_s[...]
            rr = rr_s[...] - alpha * rs
            rs_s[...] = rs
            rr_s[...] = rr
            zb = mask * smooth + beta * z_s[...]
            z_s[...] = zb
            base[...] = u - alpha * zb
            coef[...] = -(alpha * mask)

            @pl.when(k == STEPS - 1)
            def _():
                smbuf[mp] = jnp.broadcast_to(two_sums(lanes_of(r * r), lanes_of(r * rr)), (8, 128))
                sdbuf[dp] = rw_ref[...] * fr * fr
                for peer in m_peers:
                    pltpu.make_async_remote_copy(
                        src_ref=smbuf.at[mp], dst_ref=smbuf.at[mp], send_sem=s_send.at[0], recv_sem=s_recv.at[0],
                        device_id=peer, device_id_type=MESH,
                    ).start()
                for peer in d_peers:
                    pltpu.make_async_remote_copy(
                        src_ref=sdbuf.at[dp], dst_ref=sdbuf.at[dp], send_sem=s_send.at[1], recv_sem=s_recv.at[1],
                        device_id=peer, device_id_type=MESH,
                    ).start()

        pltpu.make_async_copy(all_m, all_m, m_send.at[now]).wait()
        all_d = dbuf.at[now, pl.ds(0, DP - 1)]
        pltpu.make_async_copy(all_d, all_d, d_recv.at[now]).wait()
        density = dbuf[now, 0]
        for j in range(1, 6):
            density += dbuf[now, j]
        suscept = dbuf[now, 6] + dbuf[now, 7]
        summed = jnp.stack([density[:8], suscept[:8], density[8:], suscept[8:]])
        v = base[...] + coef[...] * summed
        ubuf[later] = v
        z_s[...] = z_s[...] + jnp.where(k >= 2, mask, 0.0) * summed

        @pl.when(k < STEPS - 1)
        def _():
            product = jnp.dot(spread(chosen(v)), mt[...], preferred_element_type=F32)
            mbuf[later, mp, 0:8] = gathered(product, 0)
            r = r_s[...]
            mbuf[later, mp, 8:9] = two_sums(lanes_of(r * r), lanes_of(r * v))

        pltpu.make_async_copy(all_d, all_d, d_send.at[now]).wait()
        return carry

    r_s[...] = jnp.zeros_like(r_s)
    lax.fori_loop(0, STEPS, step, 0)

    all_sm = smbuf.at[pl.ds(0, MP - 1)]
    pltpu.make_async_copy(all_sm, all_sm, s_recv.at[0]).wait()
    all_sd = sdbuf.at[pl.ds(0, DP - 1)]
    pltpu.make_async_copy(all_sd, all_sd, s_recv.at[1]).wait()
    sums = smbuf[0]
    for j in range(1, MP):
        sums += smbuf[j]
    energy = sdbuf[0]
    for j in range(1, DP):
        energy += sdbuf[j]
    gamma, smoothed = split_sums(sums[0:1])
    delta = smoothed + jnp.sum(jnp.sum(energy, axis=0, keepdims=True), axis=1, keepdims=True)
    beta = gamma / scal[0, 0:1, 0:1]
    alpha = gamma / (delta - beta * gamma / scal[1, 0:1, 0:1])
    r = r_s[...]
    upd = x_s[...] + alpha * (r + beta * p_s[...])
    res = r - alpha * (ubuf[STEPS % 2] + beta * s_s[...])
    for layer in range(2):
        for field in range(2):
            at = pl.ds(field * 16 + layer, 8, stride=2)
            upd_ref[at, :] = upd[layer * 2 + field]
            res_ref[at, :] = res[layer * 2 + field]
    pltpu.make_async_copy(all_sm, all_sm, s_send.at[0]).wait()
    pltpu.make_async_copy(all_sd, all_sd, s_send.at[1]).wait()


def pairs(field):
    lead = field.shape[:-2]
    n = len(lead)
    cut = field.reshape(*lead, 2, 8, 128)
    return jnp.swapaxes(cut, n, n + 1).reshape(-1, 128)


def unpairs(rows):
    return jnp.swapaxes(rows.reshape(2, 8, 2, 128), 1, 2).reshape(2, 2, 1024)


def local(sensitivity, observed, row_weight, model, smooth_weight, active):
    vmem = pl.BlockSpec(memory_space=pltpu.VMEM)
    cells = pltpu.VMEM((4, 8, 128), F32)
    tile = pltpu.VMEM((8, 128), F32)
    upd, res = pl.pallas_call(
        kernel,
        out_shape=[jax.ShapeDtypeStruct((32, 128), F32)] * 2,
        in_specs=[pl.BlockSpec(memory_space=pl.ANY)] + [vmem] * 5,
        out_specs=[vmem, vmem],
        scratch_shapes=[
            pltpu.VMEM((ROWS * 16, 128), BF16),
            pltpu.VMEM((CHUNK * 16, 128), F32),
            pltpu.VMEM((ROWS, CELLS), BF16),
            pltpu.VMEM((CELLS, ROWS), BF16),
            pltpu.VMEM((2, MP, 16, 128), F32),
            pltpu.VMEM((2, DP, 16, 128), F32),
            pltpu.VMEM((2, 4, 8, 128), F32),
            pltpu.VMEM((2, 2, 2, 8, 128), F32),
            pltpu.VMEM((MP, 8, 128), F32),
            pltpu.VMEM((DP, 8, 128), F32),
            cells,
            pltpu.VMEM((2, 8, 128), F32),
            cells, cells, cells, cells, cells, cells, cells, cells, cells,
            tile, tile,
            pltpu.VMEM((2, 8, 128), F32),
            pltpu.SemaphoreType.DMA((CHUNKS,)),
            pltpu.SemaphoreType.DMA((2,)),
            pltpu.SemaphoreType.DMA((2,)),
            pltpu.SemaphoreType.DMA((2,)),
            pltpu.SemaphoreType.DMA((2,)),
            pltpu.SemaphoreType.DMA((2,)),
            pltpu.SemaphoreType.DMA((2, 2)),
            pltpu.SemaphoreType.DMA((2,)),
            pltpu.SemaphoreType.DMA((2,)),
        ],
        compiler_params=pltpu.CompilerParams(
            collective_id=0, has_side_effects=True, vmem_limit_bytes=32 * 2**20
        ),
    )(
        pairs(sensitivity),
        observed.reshape(8, 128),
        row_weight.reshape(8, 128),
        pairs(model),
        pairs(smooth_weight),
        pairs(active),
    )
    return unpairs(upd), unpairs(res)


def solution(mesh):
    return jax.shard_map(
        local,
        mesh=mesh,
        in_specs=(
            P("dp", "mp", None),
            P("dp"),
            P("dp"),
            P(None, "mp", None),
            P("mp", None),
            P(None, "mp", None),
        ),
        out_specs=(P(None, "mp", None), P(None, "mp", None)),
        check_vma=False,
    )
```

time: 287 us -> 67.5 us (0.24)
  starting transfers between devices: 93.7 us -> 0 us
  blocking collectives: 80.3 us -> 0 us
  Pallas kernels: 0 us -> 59.5 us
  waiting for transfers between devices: 37.3 us -> 0 us
  matrix products: 31.1 us -> 0 us
  local copies, waits for them, and re-layouts: 19.3 us -> 6.9 us
  other arithmetic: 11.8 us -> 0 us
  between operations: 10.6 us -> 0.65 us
    all_to_all x7 -> x0, blocking collectives: 80.3 us -> none  [from_everyone(): lax.all_to_all(jnp.broadcast_to(x[None], (count, *x.shape)), axis, 0, 0,...]
    all_to_all x11 -> x0, starting transfers between devices: 67.2 us -> none  [from_everyone(): lax.all_to_all(jnp.broadcast_to(x[None], (count, *x.shape)), axis, 0, 0,...]
    pallas_call x0 -> x1, Pallas kernels: none -> 59.5 us  [local(): pl.pallas_call(kernel, out_shape=[jax.ShapeDtypeStruct((32, 128), F32)] *...]
    all_to_all x11 -> x0, waiting for transfers between devices: 37.2 us -> none  [from_everyone(): lax.all_to_all(jnp.broadcast_to(x[None], (count, *x.shape)), axis, 0, 0,...]
    dot_general x10 -> x0, matrix products: 31.1 us -> none  [the longest x5 16.8 us: forward(): partial_rows = jnp.dot(matrix, chosen, preferred_element_type=jnp.float32)]
    ppermute x10 -> x0, starting transfers between devices: 26.6 us -> none  [the longest x5 20.1 us: with_halo(): lax.ppermute(tail, axis, [(i, (i + 1) % count) for i in range(ends)])]
    broadcast_in_dim x18 -> x0, local copies, waits for them, and re-layouts: 12.6 us -> none  [from_everyone(): jnp.broadcast_to(x[None], (count, *x.shape))]
    reduce_sum x25 -> x0, other arithmetic: 10.2 us -> none  [the longest x18 5.45 us: taken_together(): return jnp.sum(everything, axis=0)]
  transfers between devices with their start and end apart: 21 -> 0, of which waited for: 11 -> 0; matrix products, arithmetic and copies ran while one was open for 7% -> 0% of each run, Pallas kernels for 0% -> 0%
where the time goes in v1:
time: 67.5 us; the launch traced here: 67.1 us
  Pallas kernels  59.5 us (88%)
  local copies, waits for them, and re-layouts  6.9 us (10%)
    pallas_call x1, Pallas kernels, local(): pl.pallas_call(kernel, out_shape=[jax.ShapeDtypeStruct((32, 128), F32)] *...  59.5 us
    unnamed x14, local copies, waits for them, and re-layouts  6.9 us

profile of v1, /device:TPU:1, one launch (start us, length us, event | category | flops | bytes accessed | tf_op | source)
XLA Modules:
  0.0 67.1 jit_solution(2416437646570240373)
XLA Ops:
  0.6 0.0 copy-start
  0.6 2.2 %copy-done = bf16[1024,2,1024]{2,1,0:T(2,128)(2,1)S(1)} copy-done((bf16[1024,2,1024]{2,1,0:T(2,128)(2,1)S(1)}, bf16[1024,2,1024]{2,1,0:T(2,128)(2,1)}, u32[]{:S(2)}) %copy-start) | copy-done | bytes 4194328
  2.8 0.0 copy-start.1
  2.8 0.7 %copy-done.1 = f32[2,2,1024]{2,1,0:T(2,128)S(1)} copy-done((f32[2,2,1024]{2,1,0:T(2,128)S(1)}, f32[2,2,1024]{2,1,0:T(2,128)}, u32[]{:S(2)}) %copy-start.1) | copy-done | bytes 16408
  3.5 0.0 copy-start.2
  3.5 0.7 %copy-done.2 = s32[2,2,1024]{2,1,0:T(2,128)S(1)} copy-done((s32[2,2,1024]{2,1,0:T(2,128)S(1)}, s32[2,2,1024]{2,1,0:T(2,128)}, u32[]{:S(2)}) %copy-start.2) | copy-done | bytes 16408
  4.3 0.0 copy-start.3
  4.3 0.7 %copy-done.3 = f32[2,1024]{1,0:T(2,128)S(1)} copy-done((f32[2,1024]{1,0:T(2,128)S(1)}, f32[2,1024]{1,0:T(2,128)}, u32[]{:S(2)}) %copy-start.3) | copy-done | bytes 8216
  5.0 0.0 copy-start.4
  5.0 0.7 %copy-done.4 = f32[1024]{0:T(1024)S(1)} copy-done((f32[1024]{0:T(1024)S(1)}, f32[1024]{0:T(1024)}, u32[]{:S(2)}) %copy-start.4) | copy-done | bytes 4120
  5.6 0.0 copy-start.5
  5.6 0.7 %copy-done.5 = f32[1024]{0:T(1024)S(1)} copy-done((f32[1024]{0:T(1024)S(1)}, f32[1024]{0:T(1024)}, u32[]{:S(2)}) %copy-start.5) | copy-done | bytes 4120
  6.3 59.5 %shard_map.77 = (f32[32,128]{1,0:T(8,128)S(1)}, f32[32,128]{1,0:T(8,128)S(1)}) custom-call(bf16[16384,128]{1,0:T(8,128)(2,1)S(1)} %bitcast.32, f32[8,128]{1,0:T(8,128)S(1)} %bitcast.38, f32[8,128]{1,0:T(8,128)S(1)} %bitcast.39, f32[32,128]{1,0:T(8,128)S(1)} %bitcast.33, f32[16,128]{1,0:T(8,128)S(1)} %bitcast.37, s32[32,128]{1,0:T(8,128)S(1)} %bitcast.34), custom_call_target="tpu_custom_call" | custom-call | tf_op jit(solution)/shard_map/pallas_call | solution.py:339
  65.8 0.6 copy.16
  66.5 0.6 copy.17
Async XLA Ops:
  0.6 2.2 %copy-start = (bf16[1024,2,1024]{2,1,0:T(2,128)(2,1)S(1)}, bf16[1024,2,1024]{2,1,0:T(2,128)(2,1)}, u32[]{:S(2)}) copy-start(bf16[1024,2,1024]{2,1,0:T(2,128)(2,1)} %param.6) | copy-start | bytes 12582916
  2.8 0.7 %copy-start.1 = (f32[2,2,1024]{2,1,0:T(2,128)S(1)}, f32[2,2,1024]{2,1,0:T(2,128)}, u32[]{:S(2)}) copy-start(f32[2,2,1024]{2,1,0:T(2,128)} %param.9) | copy-start | bytes 49156
  3.5 0.7 %copy-start.2 = (s32[2,2,1024]{2,1,0:T(2,128)S(1)}, s32[2,2,1024]{2,1,0:T(2,128)}, u32[]{:S(2)}) copy-start(s32[2,2,1024]{2,1,0:T(2,128)} %param.11) | copy-start | bytes 49156
  4.3 0.7 %copy-start.3 = (f32[2,1024]{1,0:T(2,128)S(1)}, f32[2,1024]{1,0:T(2,128)}, u32[]{:S(2)}) copy-start(f32[2,1024]{1,0:T(2,128)} %param.10) | copy-start | bytes 24580
  5.0 0.7 %copy-start.4 = (f32[1024]{0:T(1024)S(1)}, f32[1024]{0:T(1024)}, u32[]{:S(2)}) copy-start(f32[1024]{0:T(1024)} %param.7) | copy-start | bytes 12292
  5.6 0.7 %copy-start.5 = (f32[1024]{0:T(1024)S(1)}, f32[1024]{0:T(1024)}, u32[]{:S(2)}) copy-start(f32[1024]{0:T(1024)} %param.8) | copy-start | bytes 12292

commit v2 on v1

--- a/solution.py
+++ b/solution.py
@@ -23,6 +23,13 @@
 DP = 8
 MP = 16
 MROWS = 9
+
+
+def far_first(me, outer, inner, place):
+    high, low = me // inner, lax.rem(me, inner)
+    steps = [(a, b) for a in range(outer) for b in range(inner) if a or b]
+    steps.sort(key=lambda s: -(min(s[0], outer - s[0]) + min(s[1], inner - s[1])))
+    return [place(lax.rem(high + a, outer) * inner + lax.rem(low + b, inner)) for a, b in steps]
 
 
 def spread(tiles):
@@ -90,16 +97,29 @@
 
 
 def kernel(
-    x_ref, obs_ref, rw_ref, model_ref, smooth_ref, active_ref,
-    upd_ref, res_ref,
-    raw, wide, md, mt, mbuf, dbuf, ubuf, halo, smbuf, sdbuf,
+    x_ref, obs_hbm, rw_hbm, model_hbm, smooth_hbm, active_hbm,
+    out_ref,
+    obs_ref, rw_ref, model_ref, smooth_ref, active_ref, raw, wide, md, mt, mbuf, dbuf, ubuf, halo, smbuf, sdbuf,
     free, weight, x_s, r_s, p_s, s_s, z_s, rs_s, rr_s, base, coef, fs_s, fr_s, scal,
-    load_sem, m_send, m_recv, d_send, d_recv, h_send, h_recv, s_send, s_recv,
+    small_sem, load_sem, m_send, m_recv, d_send, d_recv, h_send, h_recv, s_send, s_recv,
 ):
     dp = lax.axis_index("dp")
     mp = lax.axis_index("mp")
     gravity = dp < DP * 3 // 4
 
+    smalls = [
+        pltpu.make_async_copy(src, dst, small_sem.at[k])
+        for k, (src, dst) in enumerate(
+            [
+                (model_hbm, model_ref),
+                (active_hbm, active_ref),
+                (smooth_hbm, smooth_ref),
+                (obs_hbm, obs_ref),
+                (rw_hbm, rw_ref),
+            ]
+        )
+    ]
+    smalls[0].start()
     loads = [
         pltpu.make_async_copy(
             x_ref.at[pl.ds(k * CHUNK * 16, CHUNK * 16)],
@@ -110,19 +130,20 @@
     ]
     for load in loads:
         load.start()
-
-    m_peers = [{"dp": dp, "mp": lax.rem(mp + k, MP)} for k in range(1, MP)]
-    d_peers = [{"dp": lax.rem(dp + k, DP), "mp": mp} for k in range(1, DP)]
+    for small in smalls[1:]:
+        small.start()
+
+    m_peers = far_first(mp, MP // 4, 4, lambda other: {"dp": dp, "mp": other})
+    d_peers = far_first(dp, 4, DP // 4, lambda other: {"dp": other, "mp": mp})
     barrier = pltpu.get_barrier_semaphore()
     for peer in m_peers + d_peers:
         pl.semaphore_signal(barrier, inc=1, device_id=peer, device_id_type=MESH)
 
+    smalls[0].wait()
     for layer in range(2):
-        weight[layer] = smooth_ref[pl.ds(layer, 8, stride=2), :]
         for field in range(2):
             at = pl.ds(field * 16 + layer, 8, stride=2)
             ubuf[0, layer * 2 + field] = model_ref[at, :]
-            free[layer * 2 + field] = 1.0 - active_ref[at, :].astype(F32)
     for ref in (x_s, p_s, s_s, z_s, rs_s):
         ref[...] = jnp.zeros_like(ref)
     fs_s[...] = jnp.zeros_like(fs_s)
@@ -184,6 +205,13 @@
                 return carry
 
             lax.fori_loop(0, CELLS // 256, turn, 0)
+            for small in smalls[1:]:
+                small.wait()
+            for layer in range(2):
+                weight[layer] = smooth_ref[pl.ds(layer, 8, stride=2), :]
+                for field in range(2):
+                    at = pl.ds(field * 16 + layer, 8, stride=2)
+                    free[layer * 2 + field] = 1.0 - active_ref[at, :].astype(F32)
 
         all_m = mbuf.at[now, pl.ds(0, MP - 1), pl.ds(0, MROWS)]
         pltpu.make_async_copy(all_m, all_m, m_recv.at[now]).wait()
@@ -315,8 +343,8 @@
     for layer in range(2):
         for field in range(2):
             at = pl.ds(field * 16 + layer, 8, stride=2)
-            upd_ref[at, :] = upd[layer * 2 + field]
-            res_ref[at, :] = res[layer * 2 + field]
+            out_ref[0, at, :] = upd[layer * 2 + field]
+            out_ref[1, at, :] = res[layer * 2 + field]
     pltpu.make_async_copy(all_sm, all_sm, s_send.at[0]).wait()
     pltpu.make_async_copy(all_sd, all_sd, s_send.at[1]).wait()
 
@@ -329,19 +357,23 @@
 
 
 def unpairs(rows):
-    return jnp.swapaxes(rows.reshape(2, 8, 2, 128), 1, 2).reshape(2, 2, 1024)
+    return jnp.swapaxes(rows.reshape(2, 2, 8, 2, 128), 2, 3).reshape(2, 2, 2, 1024)
 
 
 def local(sensitivity, observed, row_weight, model, smooth_weight, active):
     vmem = pl.BlockSpec(memory_space=pltpu.VMEM)
     cells = pltpu.VMEM((4, 8, 128), F32)
     tile = pltpu.VMEM((8, 128), F32)
-    upd, res = pl.pallas_call(
+    out = pl.pallas_call(
         kernel,
-        out_shape=[jax.ShapeDtypeStruct((32, 128), F32)] * 2,
-        in_specs=[pl.BlockSpec(memory_space=pl.ANY)] + [vmem] * 5,
-        out_specs=[vmem, vmem],
+        out_shape=jax.ShapeDtypeStruct((2, 32, 128), F32),
+        in_specs=[pl.BlockSpec(memory_space=pltpu.HBM)] * 6,
+        out_specs=vmem,
         scratch_shapes=[
+            tile, tile,
+            pltpu.VMEM((32, 128), F32),
+            pltpu.VMEM((16, 128), F32),
+            pltpu.VMEM((32, 128), jnp.int32),
             pltpu.VMEM((ROWS * 16, 128), BF16),
             pltpu.VMEM((CHUNK * 16, 128), F32),
             pltpu.VMEM((ROWS, CELLS), BF16),
@@ -357,6 +389,7 @@
             cells, cells, cells, cells, cells, cells, cells, cells, cells,
             tile, tile,
             pltpu.VMEM((2, 8, 128), F32),
+            pltpu.SemaphoreType.DMA((5,)),
             pltpu.SemaphoreType.DMA((CHUNKS,)),
             pltpu.SemaphoreType.DMA((2,)),
             pltpu.SemaphoreType.DMA((2,)),
@@ -368,7 +401,7 @@
             pltpu.SemaphoreType.DMA((2,)),
         ],
         compiler_params=pltpu.CompilerParams(
-            collective_id=0, has_side_effects=True, vmem_limit_bytes=32 * 2**20
+            collective_id=0, has_side_effects=True, vmem_limit_bytes=60 * 2**20
         ),
     )(
         pairs(sensitivity),
@@ -378,7 +411,8 @@
         pairs(smooth_weight),
         pairs(active),
     )
-    return unpairs(upd), unpairs(res)
+    both = unpairs(out)
+    return both[0], both[1]
 
 
 def solution(mesh):

time: 67.5 us -> 62.2 us (0.921)
  local copies, waits for them, and re-layouts: 6.9 us -> 1.35 us
    unnamed x14 -> x0, local copies, waits for them, and re-layouts: 6.9 us -> none
    squeeze x0 -> x1, local copies, waits for them, and re-layouts: none -> 1.35 us  [local(): return (both[0], both[1])]
where the time goes in v2:
time: 62.2 us; the launch traced here: 62 us
  Pallas kernels  60.1 us (97%)
  local copies, waits for them, and re-layouts  1.35 us (2%)
  between operations  0.64 us (1%)
    pallas_call x1, Pallas kernels, local(): pl.pallas_call(kernel, out_shape=jax.ShapeDtypeStruct((2, 32, 128), F32),...  60.1 us
    squeeze x1, local copies, waits for them, and re-layouts, local(): return (both[0], both[1])  1.35 us

profile of v2, /device:TPU:1, one launch (start us, length us, event | category | flops | bytes accessed | tf_op | source)
XLA Modules:
  0.0 62.0 jit_solution(13936036379114050940)
XLA Ops:
  0.6 60.1 %shard_map.77 = f32[2,32,128]{2,1,0:T(8,128)} custom-call(bf16[16384,128]{1,0:T(8,128)(2,1)} %bitcast.29, f32[8,128]{1,0:T(8,128)} %bitcast.34, f32[8,128]{1,0:T(8,128)} %bitcast.35, f32[32,128]{1,0:T(8,128)} %bitcast.31, f32[16,128]{1,0:T(8,128)} %bitcast.33, s32[32,128]{1,0:T(8,128)} %bitcast.32), custom_call_target="tpu_custom_call" | custom-call | tf_op jit(solution)/shard_map/pallas_call | solution.py:367
  60.7 1.3 %slice_bitcast_fusion = (f32[2,2,1024]{2,1,0:T(2,128)}, f32[2,2,1024]{2,1,0:T(2,128)}) fusion(f32[2,2,2,8,128]{4,2,3,1,0:T(2,128)} %bitcast.30), kind=kLoop, calls=%fused_computation | loop fusion | bytes 65536 | tf_op jit(solution)/shard_map/squeeze | solution.py:415

commit v3 on v2

--- a/solution.py
+++ b/solution.py
@@ -18,11 +18,12 @@
 
 ROWS = 1024
 CELLS = 2048
-CHUNK = 128
+CHUNK = 64
 CHUNKS = ROWS // CHUNK
 DP = 8
 MP = 16
 MROWS = 9
+SROWS = 12
 
 
 def far_first(me, outer, inner, place):
@@ -99,7 +100,7 @@
 def kernel(
     x_ref, obs_hbm, rw_hbm, model_hbm, smooth_hbm, active_hbm,
     out_ref,
-    obs_ref, rw_ref, model_ref, smooth_ref, active_ref, raw, wide, md, mt, mbuf, dbuf, ubuf, halo, smbuf, sdbuf,
+    obs_ref, rw_ref, model_ref, smooth_ref, active_ref, raw, halves, md, mt, mbuf, dbuf, ubuf, halo, smbuf, sdbuf,
     free, weight, x_s, r_s, p_s, s_s, z_s, rs_s, rr_s, base, coef, fs_s, fr_s, scal,
     small_sem, load_sem, m_send, m_recv, d_send, d_recv, h_send, h_recv, s_send, s_recv,
 ):
@@ -147,26 +148,34 @@
     for ref in (x_s, p_s, s_s, z_s, rs_s):
         ref[...] = jnp.zeros_like(ref)
     fs_s[...] = jnp.zeros_like(fs_s)
+    sdbuf[dp] = jnp.zeros((8, 128), F32)
 
     def chosen(u):
         return [jnp.where(gravity, u[layer * 2], u[layer * 2 + 1]) for layer in range(2)]
 
-    left = spread(chosen(ubuf[0]))
+    first = chosen(ubuf[0])
     for k in range(CHUNKS):
         loads[k].wait()
-        wide[...] = raw[pl.ds(k * CHUNK * 16, CHUNK * 16), :].astype(F32)
+        block = raw[pl.ds(k * CHUNK * 16, CHUNK * 16), :].reshape(CHUNK, 16, 128)
+        turned = jnp.swapaxes(block, 0, 1)
+        acc = jnp.zeros((CHUNK, 128), F32)
         for c in range(8):
             for layer in range(2):
                 at = (layer * 8 + c) * 128
-                part = wide[pl.ds(c * 2 + layer, CHUNK, stride=16), :]
-                md[pl.ds(k * CHUNK, CHUNK), at : at + 128] = part.astype(BF16)
-        some = lax.dot_general(
-            left, md[pl.ds(k * CHUNK, CHUNK), :], (((1,), (1,)), ((), ())), preferred_element_type=F32
-        )
-        mbuf[0, mp, k : k + 1, :] = some[0:1] + some[8:9]
+                part = turned[c * 2 + layer]
+                md[pl.ds(k * CHUNK, CHUNK), at : at + 128] = part
+                acc += part.astype(F32) * first[layer][c : c + 1]
+        high = acc.astype(BF16)
+        halves[pl.ds(k * CHUNK, CHUNK), :128] = high
+        halves[pl.ds(k * CHUNK, CHUNK), 128:] = (acc - high.astype(F32)).astype(BF16)
+    ones = jnp.ones((16, 256), BF16)
+    sums = lax.dot_general(ones, halves[...], (((1,), (1,)), ((), ())), preferred_element_type=F32)
+    for c in range(8):
+        mbuf[0, mp, c : c + 1, :] = sums[0:1, c * 128 : c * 128 + 128]
     mbuf[0, mp, 8:9, :] = jnp.zeros((1, 128), F32)
 
     pl.semaphore_wait(barrier, MP - 1 + DP - 1)
+    scalar_blocks = [smbuf.at[pl.ds(0, MP - 1), pl.ds(0, SROWS)], sdbuf.at[pl.ds(0, DP - 1)]]
 
     def step(k, carry):
         now = lax.rem(k, 2)
@@ -213,6 +222,27 @@
                     at = pl.ds(field * 16 + layer, 8, stride=2)
                     free[layer * 2 + field] = 1.0 - active_ref[at, :].astype(F32)
 
+        for copy in halo_copies:
+            copy.wait()
+        u = ubuf[now]
+        below = jnp.where(mp > 0, halo[now, 0], 0.0)
+        above = jnp.where(mp < MP - 1, halo[now, 1], 0.0)
+        smooth = regular(u, below, above, weight[...])
+        mask = free[...]
+
+        @pl.when(k == STEPS - 1)
+        def _():
+            r, s, rr, rs = r_s[...], s_s[...], rr_s[...], rs_s[...]
+            pairs_of = [(r, r), (u, r), (s, r), (u, u), (u, s), (s, s), (r, rr), (u, rr), (s, rr), (u, smooth), (u, rs), (s, rs)]
+            for j, (one, two) in enumerate(pairs_of):
+                smbuf[mp, j : j + 1] = lanes_of(one * two)
+            mine_s = smbuf.at[mp, pl.ds(0, SROWS)]
+            for peer in m_peers:
+                pltpu.make_async_remote_copy(
+                    src_ref=mine_s, dst_ref=mine_s, send_sem=s_send.at[0], recv_sem=s_recv.at[0],
+                    device_id=peer, device_id_type=MESH,
+                ).start()
+
         all_m = mbuf.at[now, pl.ds(0, MP - 1), pl.ds(0, MROWS)]
         pltpu.make_async_copy(all_m, all_m, m_recv.at[now]).wait()
         rows = mbuf[now, 0, 0:8]
@@ -232,13 +262,17 @@
                 device_id=peer, device_id_type=MESH,
             ).start()
 
-        for copy in halo_copies:
-            copy.wait()
-        u = ubuf[now]
-        below = jnp.where(mp > 0, halo[now, 0], 0.0)
-        above = jnp.where(mp < MP - 1, halo[now, 1], 0.0)
-        smooth = regular(u, below, above, weight[...])
-        mask = free[...]
+        @pl.when(k == STEPS - 1)
+        def _():
+            fr, fs = fr_s[...], fs_s[...]
+            for j, (one, two) in enumerate([(fr, fr), (rows, fr), (fs, fr), (rows, rows), (rows, fs), (fs, fs)]):
+                sdbuf[dp, j : j + 1] = jnp.sum(rw_ref[...] * one * two, axis=0, keepdims=True)
+            mine_e = sdbuf.at[dp]
+            for peer in d_peers:
+                pltpu.make_async_remote_copy(
+                    src_ref=mine_e, dst_ref=mine_e, send_sem=s_send.at[1], recv_sem=s_recv.at[1],
+                    device_id=peer, device_id_type=MESH,
+                ).start()
 
         @pl.when(k == 0)
         def _():
@@ -262,6 +296,7 @@
             alpha = gamma / (delta - past)
             scal[0] = jnp.broadcast_to(gamma, (8, 128))
             scal[1] = jnp.broadcast_to(alpha, (8, 128))
+            scal[2] = jnp.broadcast_to(beta, (8, 128))
             r = r_s[...]
             p = r + beta * p_s[...]
             s = u + beta * s_s[...]
@@ -283,20 +318,34 @@
             base[...] = u - alpha * zb
             coef[...] = -(alpha * mask)
 
-            @pl.when(k == STEPS - 1)
-            def _():
-                smbuf[mp] = jnp.broadcast_to(two_sums(lanes_of(r * r), lanes_of(r * rr)), (8, 128))
-                sdbuf[dp] = rw_ref[...] * fr * fr
-                for peer in m_peers:
-                    pltpu.make_async_remote_copy(
-                        src_ref=smbuf.at[mp], dst_ref=smbuf.at[mp], send_sem=s_send.at[0], recv_sem=s_recv.at[0],
-                        device_id=peer, device_id_type=MESH,
-                    ).start()
-                for peer in d_peers:
-                    pltpu.make_async_remote_copy(
-                        src_ref=sdbuf.at[dp], dst_ref=sdbuf.at[dp], send_sem=s_send.at[1], recv_sem=s_recv.at[1],
-                        device_id=peer, device_id_type=MESH,
-                    ).start()
+        @pl.when(k == STEPS - 1)
+        def _():
+            for n, others in enumerate(scalar_blocks):
+                pltpu.make_async_copy(others, others, s_recv.at[n]).wait()
+            dots = smbuf[0, 0:SROWS]
+            for j in range(1, MP):
+                dots += smbuf[j, 0:SROWS]
+            weighed = sdbuf[0]
+            for j in range(1, DP):
+                weighed += sdbuf[j]
+            a, b, g = scal[1, 0:1, 0:1], scal[2, 0:1, 0:1], scal[0, 0:1, 0:1]
+
+            def after(rows):
+                rr, wr, sr, ww, ws, ss = (rows[j : j + 1] for j in range(6))
+                terms = rr - (2.0 * a) * (wr + b * sr) + (a * a) * (ww + (2.0 * b) * ws + (b * b) * ss)
+                return jnp.sum(terms, axis=1, keepdims=True)
+
+            gamma = after(dots[0:6])
+            delta = after(dots[6:12]) + after(weighed[0:6])
+            beta = gamma / g
+            alpha = gamma / (delta - beta * gamma / a)
+            r = r_s[...]
+            upd = x_s[...] + alpha * (r + beta * p_s[...])
+            base[...] = r - alpha * (beta * s_s[...] + base[...])
+            coef[...] = -(alpha * coef[...])
+            for layer in range(2):
+                for field in range(2):
+                    out_ref[0, pl.ds(field * 16 + layer, 8, stride=2), :] = upd[layer * 2 + field]
 
         pltpu.make_async_copy(all_m, all_m, m_send.at[now]).wait()
         all_d = dbuf.at[now, pl.ds(0, DP - 1)]
@@ -323,30 +372,12 @@
     r_s[...] = jnp.zeros_like(r_s)
     lax.fori_loop(0, STEPS, step, 0)
 
-    all_sm = smbuf.at[pl.ds(0, MP - 1)]
-    pltpu.make_async_copy(all_sm, all_sm, s_recv.at[0]).wait()
-    all_sd = sdbuf.at[pl.ds(0, DP - 1)]
-    pltpu.make_async_copy(all_sd, all_sd, s_recv.at[1]).wait()
-    sums = smbuf[0]
-    for j in range(1, MP):
-        sums += smbuf[j]
-    energy = sdbuf[0]
-    for j in range(1, DP):
-        energy += sdbuf[j]
-    gamma, smoothed = split_sums(sums[0:1])
-    delta = smoothed + jnp.sum(jnp.sum(energy, axis=0, keepdims=True), axis=1, keepdims=True)
-    beta = gamma / scal[0, 0:1, 0:1]
-    alpha = gamma / (delta - beta * gamma / scal[1, 0:1, 0:1])
-    r = r_s[...]
-    upd = x_s[...] + alpha * (r + beta * p_s[...])
-    res = r - alpha * (ubuf[STEPS % 2] + beta * s_s[...])
+    res = ubuf[STEPS % 2]
     for layer in range(2):
         for field in range(2):
-            at = pl.ds(field * 16 + layer, 8, stride=2)
-            out_ref[0, at, :] = upd[layer * 2 + field]
-            out_ref[1, at, :] = res[layer * 2 + field]
-    pltpu.make_async_copy(all_sm, all_sm, s_send.at[0]).wait()
-    pltpu.make_async_copy(all_sd, all_sd, s_send.at[1]).wait()
+            out_ref[1, pl.ds(field * 16 + layer, 8, stride=2), :] = res[layer * 2 + field]
+    for n, others in enumerate(scalar_blocks):
+        pltpu.make_async_copy(others, others, s_send.at[n]).wait()
 
 
 def pairs(field):
@@ -375,20 +406,20 @@
             pltpu.VMEM((16, 128), F32),
             pltpu.VMEM((32, 128), jnp.int32),
             pltpu.VMEM((ROWS * 16, 128), BF16),
-            pltpu.VMEM((CHUNK * 16, 128), F32),
+            pltpu.VMEM((ROWS, 256), BF16),
             pltpu.VMEM((ROWS, CELLS), BF16),
             pltpu.VMEM((CELLS, ROWS), BF16),
             pltpu.VMEM((2, MP, 16, 128), F32),
             pltpu.VMEM((2, DP, 16, 128), F32),
             pltpu.VMEM((2, 4, 8, 128), F32),
             pltpu.VMEM((2, 2, 2, 8, 128), F32),
-            pltpu.VMEM((MP, 8, 128), F32),
+            pltpu.VMEM((MP, 16, 128), F32),
             pltpu.VMEM((DP, 8, 128), F32),
             cells,
             pltpu.VMEM((2, 8, 128), F32),
             cells, cells, cells, cells, cells, cells, cells, cells, cells,
             tile, tile,
-            pltpu.VMEM((2, 8, 128), F32),
+            pltpu.VMEM((3, 8, 128), F32),
             pltpu.SemaphoreType.DMA((5,)),
             pltpu.SemaphoreType.DMA((CHUNKS,)),
             pltpu.SemaphoreType.DMA((2,)),

time: 62.2 us -> 61.2 us (0.984)
  Pallas kernels: 60.1 us -> 59.1 us
    pallas_call x1, Pallas kernels: 60.1 us -> 59.1 us  [local(): pl.pallas_call(kernel, out_shape=jax.ShapeDtypeStruct((2, 32, 128), F32),...]
where the time goes in v3:
time: 61.2 us; the launch traced here: 61 us
  Pallas kernels  59.1 us (97%)
  local copies, waits for them, and re-layouts  1.35 us (2%)
  between operations  0.64 us (1%)
    pallas_call x1, Pallas kernels, local(): pl.pallas_call(kernel, out_shape=jax.ShapeDtypeStruct((2, 32, 128), F32),...  59.1 us
    squeeze x1, local copies, waits for them, and re-layouts, local(): return (both[0], both[1])  1.35 us

profile of v3, /device:TPU:1, one launch (start us, length us, event | category | flops | bytes accessed | tf_op | source)
XLA Modules:
  0.0 61.0 jit_solution(2527962867887760466)
XLA Ops:
  0.6 59.1 %shard_map.77 = f32[2,32,128]{2,1,0:T(8,128)} custom-call(bf16[16384,128]{1,0:T(8,128)(2,1)} %bitcast.29, f32[8,128]{1,0:T(8,128)} %bitcast.34, f32[8,128]{1,0:T(8,128)} %bitcast.35, f32[32,128]{1,0:T(8,128)} %bitcast.31, f32[16,128]{1,0:T(8,128)} %bitcast.33, s32[32,128]{1,0:T(8,128)} %bitcast.32), custom_call_target="tpu_custom_call" | custom-call | tf_op jit(solution)/shard_map/pallas_call | solution.py:398
  59.7 1.3 %slice_bitcast_fusion = (f32[2,2,1024]{2,1,0:T(2,128)}, f32[2,2,1024]{2,1,0:T(2,128)}) fusion(f32[2,2,2,8,128]{4,2,3,1,0:T(2,128)} %bitcast.30), kind=kLoop, calls=%fused_computation | loop fusion | bytes 65536 | tf_op jit(solution)/shard_map/squeeze | solution.py:446

commit v4 on v3

--- a/solution.py
+++ b/solution.py
@@ -50,13 +50,28 @@
     return jnp.concatenate(parts, axis=1)
 
 
-def gathered(product, first):
-    total = product[:8] + product[8:]
+def product(tiles, matrix, split):
+    width = matrix.shape[1]
+    sums = [None] * ((width - split) // 128)
+    for q in range(matrix.shape[0] // 128):
+        row = tiles[q // 8][q % 8 : q % 8 + 1]
+        column = jnp.transpose(jnp.broadcast_to(row, (128, 128)))
+        for j in range(len(sums)):
+            at = split + j * 128
+            term = matrix[pl.ds(q * 128, 128), at : at + 128].astype(F32) * column
+            term = jnp.sum(term.reshape(16, 8, 128), axis=0)
+            sums[j] = term if sums[j] is None else sums[j] + term
+    both = jnp.dot(spread(tiles), matrix[:, :split], preferred_element_type=F32)
+    total = both[:8] + both[8:]
+    outs = [total[:, at : at + 128] for at in range(0, split, 128)]
+    return outs + [jnp.broadcast_to(jnp.sum(one, axis=0, keepdims=True), (8, 128)) for one in sums]
+
+
+def gathered(outs):
     sub = lax.broadcasted_iota(jnp.int32, (8, 128), 0)
-    tile = jnp.zeros((8, 128), F32)
-    for c in range(8):
-        at = (first + c) * 128
-        tile = jnp.where(sub == c, total[:, at : at + 128], tile)
+    tile = outs[0]
+    for c in range(1, 8):
+        tile = jnp.where(sub == c, outs[c], tile)
     return tile
 
 
@@ -101,7 +116,7 @@
     x_ref, obs_hbm, rw_hbm, model_hbm, smooth_hbm, active_hbm,
     out_ref,
     obs_ref, rw_ref, model_ref, smooth_ref, active_ref, raw, halves, md, mt, mbuf, dbuf, ubuf, halo, smbuf, sdbuf,
-    free, weight, x_s, r_s, p_s, s_s, z_s, rs_s, rr_s, base, coef, fs_s, fr_s, scal,
+    free, weight, smooth_s, x_s, r_s, p_s, s_s, z_s, rs_s, rr_s, base, coef, fs_s, fr_s, scal,
     small_sem, load_sem, m_send, m_recv, d_send, d_recv, h_send, h_recv, s_send, s_recv,
 ):
     dp = lax.axis_index("dp")
@@ -153,18 +168,20 @@
     def chosen(u):
         return [jnp.where(gravity, u[layer * 2], u[layer * 2 + 1]) for layer in range(2)]
 
-    first = chosen(ubuf[0])
+    first = [tile.astype(BF16) for tile in chosen(ubuf[0])]
     for k in range(CHUNKS):
         loads[k].wait()
         block = raw[pl.ds(k * CHUNK * 16, CHUNK * 16), :].reshape(CHUNK, 16, 128)
         turned = jnp.swapaxes(block, 0, 1)
         acc = jnp.zeros((CHUNK, 128), F32)
         for c in range(8):
+            terms = []
             for layer in range(2):
                 at = (layer * 8 + c) * 128
                 part = turned[c * 2 + layer]
                 md[pl.ds(k * CHUNK, CHUNK), at : at + 128] = part
-                acc += part.astype(F32) * first[layer][c : c + 1]
+                terms.append(part * first[layer][c : c + 1])
+            acc += (terms[0] + terms[1]).astype(F32)
         high = acc.astype(BF16)
         halves[pl.ds(k * CHUNK, CHUNK), :128] = high
         halves[pl.ds(k * CHUNK, CHUNK), 128:] = (acc - high.astype(F32)).astype(BF16)
@@ -222,16 +239,21 @@
                     at = pl.ds(field * 16 + layer, 8, stride=2)
                     free[layer * 2 + field] = 1.0 - active_ref[at, :].astype(F32)
 
-        for copy in halo_copies:
-            copy.wait()
         u = ubuf[now]
-        below = jnp.where(mp > 0, halo[now, 0], 0.0)
-        above = jnp.where(mp < MP - 1, halo[now, 1], 0.0)
-        smooth = regular(u, below, above, weight[...])
         mask = free[...]
 
+        def regularize():
+            for copy in halo_copies:
+                copy.wait()
+            below = jnp.where(mp > 0, halo[now, 0], 0.0)
+            above = jnp.where(mp < MP - 1, halo[now, 1], 0.0)
+            smooth = regular(u, below, above, weight[...])
+            smooth_s[...] = smooth
+            return smooth
+
         @pl.when(k == STEPS - 1)
         def _():
+            smooth = regularize()
             r, s, rr, rs = r_s[...], s_s[...], rr_s[...], rs_s[...]
             pairs_of = [(r, r), (u, r), (s, r), (u, u), (u, s), (s, s), (r, rr), (u, rr), (s, rr), (u, smooth), (u, rs), (s, rs)]
             for j, (one, two) in enumerate(pairs_of):
@@ -252,15 +274,19 @@
             sums += mbuf[now, j, 8:9]
 
         scaled = rw_ref[...] * (rows - jnp.where(k == 0, obs_ref[...], 0.0))
-        product = jnp.dot(spread([scaled]), md[...], preferred_element_type=F32)
-        dbuf[now, dp, 0:8] = gathered(product, 0)
-        dbuf[now, dp, 8:16] = gathered(product, 8)
+        columns = product([scaled], md, CELLS - 512)
+        dbuf[now, dp, 0:8] = gathered(columns[:8])
+        dbuf[now, dp, 8:16] = gathered(columns[8:])
         mine_d = dbuf.at[now, dp]
         for peer in d_peers:
             pltpu.make_async_remote_copy(
                 src_ref=mine_d, dst_ref=mine_d, send_sem=d_send.at[now], recv_sem=d_recv.at[now],
                 device_id=peer, device_id_type=MESH,
             ).start()
+
+        @pl.when(k < STEPS - 1)
+        def _():
+            regularize()
 
         @pl.when(k == STEPS - 1)
         def _():
@@ -273,6 +299,8 @@
                     src_ref=mine_e, dst_ref=mine_e, send_sem=s_send.at[1], recv_sem=s_recv.at[1],
                     device_id=peer, device_id_type=MESH,
                 ).start()
+
+        smooth = smooth_s[...]
 
         @pl.when(k == 0)
         def _():
@@ -361,8 +389,7 @@
 
         @pl.when(k < STEPS - 1)
         def _():
-            product = jnp.dot(spread(chosen(v)), mt[...], preferred_element_type=F32)
-            mbuf[later, mp, 0:8] = gathered(product, 0)
+            mbuf[later, mp, 0:8] = gathered(product(chosen(v), mt, ROWS - 256))
             r = r_s[...]
             mbuf[later, mp, 8:9] = two_sums(lanes_of(r * r), lanes_of(r * v))
 
@@ -417,7 +444,7 @@
             pltpu.VMEM((DP, 8, 128), F32),
             cells,
             pltpu.VMEM((2, 8, 128), F32),
-            cells, cells, cells, cells, cells, cells, cells, cells, cells,
+            cells, cells, cells, cells, cells, cells, cells, cells, cells, cells,
             tile, tile,
             pltpu.VMEM((3, 8, 128), F32),
             pltpu.SemaphoreType.DMA((5,)),
@@ -432,15 +459,20 @@
             pltpu.SemaphoreType.DMA((2,)),
         ],
         compiler_params=pltpu.CompilerParams(
-            collective_id=0, has_side_effects=True, vmem_limit_bytes=60 * 2**20
+            collective_id=0, has_side_effects=True, vmem_limit_bytes=32 * 2**20
         ),
     )(
-        pairs(sensitivity),
-        observed.reshape(8, 128),
-        row_weight.reshape(8, 128),
-        pairs(model),
-        pairs(smooth_weight),
-        pairs(active),
+        *(
+            pltpu.with_memory_space_constraint(x, pltpu.HBM)
+            for x in (
+                pairs(sensitivity),
+                observed.reshape(8, 128),
+                row_weight.reshape(8, 128),
+                pairs(model),
+                pairs(smooth_weight),
+                pairs(active),
+            )
+        )
     )
     both = unpairs(out)
     return both[0], both[1]

time: 61.2 us -> 57.9 us (0.946)
  Pallas kernels: 59.1 us -> 56.5 us
  local copies, waits for them, and re-layouts: 1.35 us -> 0.61 us
    pallas_call x1, Pallas kernels: 59.1 us -> 56.5 us  [local(): pl.pallas_call(kernel, out_shape=jax.ShapeDtypeStruct((2, 32, 128), F32),...]
    squeeze x1, local copies, waits for them, and re-layouts: 1.35 us -> 0.61 us  [local(): return (both[0], both[1])]
where the time goes in v4:
time: 57.9 us; the launch traced here: 57.8 us
  Pallas kernels  56.5 us (98%)
  between operations  0.64 us (1%)
  local copies, waits for them, and re-layouts  0.61 us (1%)
    pallas_call x1, Pallas kernels, local(): pl.pallas_call(kernel, out_shape=jax.ShapeDtypeStruct((2, 32, 128), F32),...  56.5 us

profile of v4, /device:TPU:1, one launch (start us, length us, event | category | flops | bytes accessed | tf_op | source)
XLA Modules:
  0.0 57.8 jit_solution(5702978792566888393)
XLA Ops:
  0.6 56.5 %shard_map.77 = f32[2,32,128]{2,1,0:T(8,128)S(1)} custom-call(bf16[16384,128]{1,0:T(8,128)(2,1)} %bitcast.30, f32[8,128]{1,0:T(8,128)} %bitcast.34, f32[8,128]{1,0:T(8,128)} %bitcast.35, f32[32,128]{1,0:T(8,128)} %bitcast.31, f32[16,128]{1,0:T(8,128)} %bitcast.33, s32[32,128]{1,0:T(8,128)} %bitcast.32), custom_call_target="tpu_custom_call" | custom-call | tf_op jit(solution)/shard_map/pallas_call | solution.py:425
  57.1 0.6 %slice_bitcast_fusion = (f32[2,2,1024]{2,1,0:T(2,128)}, f32[2,2,1024]{2,1,0:T(2,128)}) fusion(f32[2,2,2,8,128]{4,2,3,1,0:T(2,128)S(1)} %bitcast.29), kind=kLoop, calls=%fused_computation | loop fusion | bytes 65536 | tf_op jit(solution)/shard_map/squeeze | solution.py:478

commit v5 on v4

--- a/solution.py
+++ b/solution.py
@@ -18,7 +18,7 @@
 
 ROWS = 1024
 CELLS = 2048
-CHUNK = 64
+CHUNK = 128
 CHUNKS = ROWS // CHUNK
 DP = 8
 MP = 16
@@ -73,6 +73,15 @@
     for c in range(1, 8):
         tile = jnp.where(sub == c, outs[c], tile)
     return tile
+
+
+def fold(one, two, gap):
+    upper = lax.broadcasted_iota(jnp.int32, (8, 128), 0) // gap % 2 == 1
+    kept = jnp.where(upper, two, one)
+    moved = jnp.where(upper, one, two)
+    if gap == 4:
+        return kept + pltpu.roll(moved, 4, 0)
+    return kept + jnp.where(upper, pltpu.roll(moved, gap, 0), pltpu.roll(moved, 8 - gap, 0))
 
 
 def regular(u, below, above, weight):
@@ -123,6 +132,12 @@
     mp = lax.axis_index("mp")
     gravity = dp < DP * 3 // 4
 
+    m_peers = far_first(mp, MP // 4, 4, lambda other: {"dp": dp, "mp": other})
+    d_peers = far_first(dp, 4, DP // 4, lambda other: {"dp": other, "mp": mp})
+    barrier = pltpu.get_barrier_semaphore()
+    for peer in m_peers + d_peers:
+        pl.semaphore_signal(barrier, inc=1, device_id=peer, device_id_type=MESH)
+
     smalls = [
         pltpu.make_async_copy(src, dst, small_sem.at[k])
         for k, (src, dst) in enumerate(
@@ -136,24 +151,14 @@
         )
     ]
     smalls[0].start()
-    loads = [
-        pltpu.make_async_copy(
-            x_ref.at[pl.ds(k * CHUNK * 16, CHUNK * 16)],
-            raw.at[pl.ds(k * CHUNK * 16, CHUNK * 16)],
-            load_sem.at[k],
-        )
-        for k in range(CHUNKS)
-    ]
-    for load in loads:
-        load.start()
+    def load(k):
+        at = pl.ds(pl.multiple_of(k * (CHUNK * 16), CHUNK * 16), CHUNK * 16)
+        return pltpu.make_async_copy(x_ref.at[at], raw.at[at], load_sem.at[k])
+
+    for k in range(CHUNKS):
+        load(k).start()
     for small in smalls[1:]:
         small.start()
-
-    m_peers = far_first(mp, MP // 4, 4, lambda other: {"dp": dp, "mp": other})
-    d_peers = far_first(dp, 4, DP // 4, lambda other: {"dp": other, "mp": mp})
-    barrier = pltpu.get_barrier_semaphore()
-    for peer in m_peers + d_peers:
-        pl.semaphore_signal(barrier, inc=1, device_id=peer, device_id_type=MESH)
 
     smalls[0].wait()
     for layer in range(2):
@@ -168,23 +173,29 @@
     def chosen(u):
         return [jnp.where(gravity, u[layer * 2], u[layer * 2 + 1]) for layer in range(2)]
 
-    first = [tile.astype(BF16) for tile in chosen(ubuf[0])]
-    for k in range(CHUNKS):
-        loads[k].wait()
-        block = raw[pl.ds(k * CHUNK * 16, CHUNK * 16), :].reshape(CHUNK, 16, 128)
-        turned = jnp.swapaxes(block, 0, 1)
-        acc = jnp.zeros((CHUNK, 128), F32)
-        for c in range(8):
-            terms = []
-            for layer in range(2):
-                at = (layer * 8 + c) * 128
-                part = turned[c * 2 + layer]
-                md[pl.ds(k * CHUNK, CHUNK), at : at + 128] = part
-                terms.append(part * first[layer][c : c + 1])
-            acc += (terms[0] + terms[1]).astype(F32)
-        high = acc.astype(BF16)
-        halves[pl.ds(k * CHUNK, CHUNK), :128] = high
-        halves[pl.ds(k * CHUNK, CHUNK), 128:] = (acc - high.astype(F32)).astype(BF16)
+    first = jnp.where(gravity, model_ref[0:16, :], model_ref[16:32, :]).astype(BF16)
+
+    def multiply(k, carry):
+        load(k).wait()
+        for group in range(CHUNK // 16):
+            folded = []
+            for half in range(2):
+                rows = []
+                for r in range(8):
+                    at = k * CHUNK + group * 16 + half * 8 + r
+                    terms = (raw[pl.ds(pl.multiple_of(at * 16, 16), 16), :] * first).astype(F32)
+                    rows.append(terms[:8] + terms[8:])
+                for gap in (4, 2, 1):
+                    rows = [fold(rows[j], rows[j + gap], gap) for j in range(gap)]
+                folded.append(rows[0])
+            acc = jnp.concatenate(folded, axis=0)
+            here = pl.ds(pl.multiple_of(k * CHUNK + group * 16, 16), 16)
+            high = acc.astype(BF16)
+            halves[here, :128] = high
+            halves[here, 128:] = (acc - high.astype(F32)).astype(BF16)
+        return carry
+
+    lax.fori_loop(0, CHUNKS, multiply, 0)
     ones = jnp.ones((16, 256), BF16)
     sums = lax.dot_general(ones, halves[...], (((1,), (1,)), ((), ())), preferred_element_type=F32)
     for c in range(8):
@@ -216,8 +227,7 @@
             copy.start()
             halo_copies.append(copy)
 
-        @pl.when(k == 0)
-        def _():
+        def turn_some(low, high):
             row = lax.broadcasted_iota(jnp.int32, (256, 256), 0)
             col = lax.broadcasted_iota(jnp.int32, (256, 256), 1)
             eye = jnp.where(row == col, 1.0, 0.0).astype(BF16)
@@ -230,7 +240,21 @@
                 mt[pl.ds(at, 256), :] = turned.astype(BF16)
                 return carry
 
-            lax.fori_loop(0, CELLS // 256, turn, 0)
+            lax.fori_loop(low, high, turn, 0)
+
+        @pl.when(k == 0)
+        def _():
+            def arrange(j, carry):
+                block = raw[pl.ds(pl.multiple_of(j * 2048, 2048), 2048), :].reshape(128, 16, 128)
+                turned = jnp.swapaxes(block, 0, 1)
+                for c in range(8):
+                    for layer in range(2):
+                        at = (layer * 8 + c) * 128
+                        md[pl.ds(pl.multiple_of(j * 128, 128), 128), at : at + 128] = turned[c * 2 + layer]
+                return carry
+
+            lax.fori_loop(0, ROWS // 128, arrange, 0)
+            turn_some(0, CELLS // 512)
             for small in smalls[1:]:
                 small.wait()
             for layer in range(2):
@@ -287,6 +311,10 @@
         @pl.when(k < STEPS - 1)
         def _():
             regularize()
+
+        @pl.when(k == 0)
+        def _():
+            turn_some(CELLS // 512, CELLS // 256)
 
         @pl.when(k == STEPS - 1)
         def _():

time: 57.9 us -> 57.2 us (0.988)
  Pallas kernels: 56.5 us -> 55.8 us
    pallas_call x1, Pallas kernels: 56.5 us -> 55.8 us  [local(): pl.pallas_call(kernel, out_shape=jax.ShapeDtypeStruct((2, 32, 128), F32),...]
where the time goes in v5:
time: 57.2 us; the launch traced here: 57.1 us
  Pallas kernels  55.8 us (98%)
  between operations  0.64 us (1%)
  local copies, waits for them, and re-layouts  0.61 us (1%)
    pallas_call x1, Pallas kernels, local(): pl.pallas_call(kernel, out_shape=jax.ShapeDtypeStruct((2, 32, 128), F32),...  55.8 us

profile of v5, /device:TPU:1, one launch (start us, length us, event | category | flops | bytes accessed | tf_op | source)
XLA Modules:
  0.0 57.1 jit_solution(17329849216344041675)
XLA Ops:
  0.6 55.8 %shard_map.77 = f32[2,32,128]{2,1,0:T(8,128)S(1)} custom-call(bf16[16384,128]{1,0:T(8,128)(2,1)} %bitcast.30, f32[8,128]{1,0:T(8,128)} %bitcast.34, f32[8,128]{1,0:T(8,128)} %bitcast.35, f32[32,128]{1,0:T(8,128)} %bitcast.31, f32[16,128]{1,0:T(8,128)} %bitcast.33, s32[32,128]{1,0:T(8,128)} %bitcast.32), custom_call_target="tpu_custom_call" | custom-call | tf_op jit(solution)/shard_map/pallas_call | solution.py:453
  56.5 0.6 %slice_bitcast_fusion = (f32[2,2,1024]{2,1,0:T(2,128)}, f32[2,2,1024]{2,1,0:T(2,128)}) fusion(f32[2,2,2,8,128]{4,2,3,1,0:T(2,128)S(1)} %bitcast.29), kind=kLoop, calls=%fused_computation | loop fusion | bytes 65536 | tf_op jit(solution)/shard_map/squeeze | solution.py:506

commit v6 on v5

--- a/solution.py
+++ b/solution.py
@@ -29,7 +29,7 @@
 def far_first(me, outer, inner, place):
     high, low = me // inner, lax.rem(me, inner)
     steps = [(a, b) for a in range(outer) for b in range(inner) if a or b]
-    steps.sort(key=lambda s: -(min(s[0], outer - s[0]) + min(s[1], inner - s[1])))
+    steps.sort(key=lambda s: (-(min(s[0], outer - s[0]) + min(s[1], inner - s[1])), s[0] + s[1] > 4, s[1]))
     return [place(lax.rem(high + a, outer) * inner + lax.rem(low + b, inner)) for a, b in steps]
 
 

time: 57.2 us -> 56.8 us (level)
  no operation moved by 1% of the time
where the time goes in v6:
time: 56.8 us; the launch traced here: 56.7 us
  Pallas kernels  55.4 us (98%)
  between operations  0.64 us (1%)
  local copies, waits for them, and re-layouts  0.61 us (1%)
    pallas_call x1, Pallas kernels, local(): pl.pallas_call(kernel, out_shape=jax.ShapeDtypeStruct((2, 32, 128), F32),...  55.4 us

profile of v6, /device:TPU:1, one launch (start us, length us, event | category | flops | bytes accessed | tf_op | source)
XLA Modules:
  0.0 56.7 jit_solution(10302836214540101470)
XLA Ops:
  0.6 55.4 %shard_map.77 = f32[2,32,128]{2,1,0:T(8,128)S(1)} custom-call(bf16[16384,128]{1,0:T(8,128)(2,1)} %bitcast.30, f32[8,128]{1,0:T(8,128)} %bitcast.34, f32[8,128]{1,0:T(8,128)} %bitcast.35, f32[32,128]{1,0:T(8,128)} %bitcast.31, f32[16,128]{1,0:T(8,128)} %bitcast.33, s32[32,128]{1,0:T(8,128)} %bitcast.32), custom_call_target="tpu_custom_call" | custom-call | tf_op jit(solution)/shard_map/pallas_call | solution.py:453
  56.1 0.6 %slice_bitcast_fusion = (f32[2,2,1024]{2,1,0:T(2,128)}, f32[2,2,1024]{2,1,0:T(2,128)}) fusion(f32[2,2,2,8,128]{4,2,3,1,0:T(2,128)S(1)} %bitcast.29), kind=kLoop, calls=%fused_computation | loop fusion | bytes 65536 | tf_op jit(solution)/shard_map/squeeze | solution.py:506

commit v7 on v5

--- a/solution.py
+++ b/solution.py
@@ -18,7 +18,7 @@
 
 ROWS = 1024
 CELLS = 2048
-CHUNK = 128
+CHUNK = 256
 CHUNKS = ROWS // CHUNK
 DP = 8
 MP = 16

time: 57.2 us -> 57.1 us (level)
  no operation moved by 1% of the time
where the time goes in v7:
time: 57.1 us; the launch traced here: 57 us
  Pallas kernels  55.7 us (98%)
  between operations  0.64 us (1%)
  local copies, waits for them, and re-layouts  0.61 us (1%)
    pallas_call x1, Pallas kernels, local(): pl.pallas_call(kernel, out_shape=jax.ShapeDtypeStruct((2, 32, 128), F32),...  55.7 us

profile of v7, /device:TPU:1, one launch (start us, length us, event | category | flops | bytes accessed | tf_op | source)
XLA Modules:
  0.0 57.0 jit_solution(2321887627500658490)
XLA Ops:
  0.6 55.7 %shard_map.77 = f32[2,32,128]{2,1,0:T(8,128)S(1)} custom-call(bf16[16384,128]{1,0:T(8,128)(2,1)} %bitcast.30, f32[8,128]{1,0:T(8,128)} %bitcast.34, f32[8,128]{1,0:T(8,128)} %bitcast.35, f32[32,128]{1,0:T(8,128)} %bitcast.31, f32[16,128]{1,0:T(8,128)} %bitcast.33, s32[32,128]{1,0:T(8,128)} %bitcast.32), custom_call_target="tpu_custom_call" | custom-call | tf_op jit(solution)/shard_map/pallas_call | solution.py:453
  56.3 0.6 %slice_bitcast_fusion = (f32[2,2,1024]{2,1,0:T(2,128)}, f32[2,2,1024]{2,1,0:T(2,128)}) fusion(f32[2,2,2,8,128]{4,2,3,1,0:T(2,128)S(1)} %bitcast.29), kind=kLoop, calls=%fused_computation | loop fusion | bytes 65536 | tf_op jit(solution)/shard_map/squeeze | solution.py:506
